TPU v7x, 256 devices: a whole 4x4x8 slice. The times are simulated.
256 devices in a mesh: exp: 64 (over y, z, core), pair: 4 (over x).
Axes of the slice: x: 4, y: 4, z: 8, core: 2. Of those that a mesh axis runs over, the one named last changes fastest.
Arguments:
- teacher_in: bfloat16 [16384, 7168], P('exp', 'pair'), may hold values from -6 to 6
- expert_ids: int32 [16384, 8], P('exp'), may hold values from 0 to 255, all different within a row; in each aligned block of 256 rows (0 to 255, 256 to 511, ...) at most 8 rows name the same one
- gate_codes: int32 [16384, 8], P('exp'), may hold values from 1 to 256
- w_gate: bfloat16 [7168, 32768], P('pair', 'exp'), may hold values from -0.0625 to 0.0625
- w_up: bfloat16 [7168, 32768], P('pair', 'exp'), may hold values from -0.0625 to 0.0625
- w_down: bfloat16 [32768, 7168], P('exp', 'pair'), may hold values from -0.125 to 0.125
- student_in: bfloat16 [16384, 2048], P('exp'), may hold values from -16 to 16
- projection: bfloat16 [2048, 7168], P('exp', 'pair'), may hold values from -0.125 to 0.125
Outputs:
- target: bfloat16 [16384, 7168], P('exp', 'pair')
- grad_projection: float32 [2048, 7168], P('exp', 'pair')
Inputs may be any that keep to these rules, and one draw needn't show every extreme that they name: `expert_ids`: each row names 8 different experts. Within each aligned block of 256 rows no expert is named by more than 8 rows, and in every draw some expert is named by exactly 8 rows of some block.
All inputs are finite; a program needn't handle non-finite values.
Results may differ from a plain program's by a relative error of at most 0.0057.
Values may be sent and summed in bfloat16 or wider, within the bound.
A program may use at most 128 MiB of HBM per device.

v0:
```python
import jax
import jax.numpy as jnp
from jax import lax
from jax.sharding import PartitionSpec as P

CAP = 8


loss_scale = 128.0
norm_epsilon = 1e-06


def body(teacher_in, expert_ids, gate_codes, w_gate, w_up, w_down, student_in, projection):
    n_exp = lax.axis_size("exp")
    groups = n_exp // 4
    tok_rows = teacher_in.shape[0]
    width = teacher_in.shape[1]
    top_k = expert_ids.shape[1]
    slots = CAP
    flat_ids = expert_ids.reshape(tok_rows * top_k)
    onehot = (flat_ids[:, None] == jnp.arange(groups, dtype=jnp.int32)[None, :]).astype(jnp.int32)
    ranks = jnp.cumsum(onehot, axis=0) - onehot
    slot_of = jnp.where(onehot == 1, ranks, -1)
    matches = (slot_of[:, :, None] == jnp.arange(slots, dtype=jnp.int32)[None, None, :]).astype(
        jnp.float32
    )
    matches = matches.reshape(tok_rows, top_k, groups * slots)
    codes = gate_codes.astype(jnp.float32) / 256.0
    chosen = jnp.sum(matches, axis=1).astype(jnp.bfloat16)
    weigh = jnp.sum(matches * codes[:, :, None], axis=1).astype(jnp.bfloat16)
    packed = lax.dot_general(
        chosen, teacher_in, (((0,), (0,)), ((), ())), preferred_element_type=jnp.float32
    )
    packed = packed.astype(jnp.bfloat16).reshape(groups, slots, width)
    outgoing = jnp.broadcast_to(packed[:, None], (groups, 4, slots, width)).reshape(
        n_exp, slots, width
    )
    arrived = lax.all_to_all(outgoing, "exp", split_axis=0, concat_axis=0, tiled=True)
    rows = arrived.reshape(n_exp * slots, width)
    gate_part = jnp.dot(rows, w_gate, preferred_element_type=jnp.float32)
    up_part = jnp.dot(rows, w_up, preferred_element_type=jnp.float32)
    gate_pre, up_pre = (
        lax.psum_scatter(gate_part, "pair", scatter_dimension=0, tiled=True),
        lax.psum_scatter(up_part, "pair", scatter_dimension=0, tiled=True),
    )
    active = lax.all_gather(
        (jax.nn.silu(gate_pre) * up_pre).astype(jnp.bfloat16), "pair", axis=0, tiled=True
    )
    produced = jnp.dot(active, w_down, preferred_element_type=jnp.float32).astype(jnp.bfloat16)
    produced = produced.reshape(n_exp, slots, width)
    returned = lax.all_to_all(produced, "exp", split_axis=0, concat_axis=0, tiled=True)
    spread = jnp.broadcast_to(
        weigh.reshape(tok_rows, groups, 1, slots), (tok_rows, groups, 4, slots)
    )
    spread = spread.reshape(tok_rows, n_exp * slots)
    target = jnp.dot(
        spread, returned.reshape(n_exp * slots, width), preferred_element_type=jnp.float32
    ).astype(jnp.bfloat16)
    wide = student_in.astype(jnp.float32)
    scale = 1.0 / jnp.sqrt(jnp.mean(wide * wide, axis=1, keepdims=True) + norm_epsilon)
    normed = (wide * scale).astype(jnp.bfloat16)
    columns = normed
    student_out = jnp.dot(
        columns,
        lax.all_gather(projection, "exp", axis=0, tiled=True),
        preferred_element_type=jnp.float32,
    )
    resid = ((student_out - target.astype(jnp.float32)) * (loss_scale / (tok_rows * n_exp))).astype(
        jnp.bfloat16
    )
    columns = normed
    grad_projection = lax.psum_scatter(
        lax.dot_general(
            columns, resid, (((0,), (0,)), ((), ())), preferred_element_type=jnp.float32
        ),
        "exp",
        scatter_dimension=0,
        tiled=True,
    )
    return (target, grad_projection)


def solution(mesh):
    in_specs = (
        P("exp", "pair"),
        P("exp", None),
        P("exp", None),
        P("pair", "exp"),
        P("pair", "exp"),
        P("exp", "pair"),
        P("exp", None),
        P("exp", "pair"),
    )
    out_specs = (P("exp", "pair"), P("exp", "pair"))
    return jax.shard_map(body, mesh=mesh, in_specs=in_specs, out_specs=out_specs, check_vma=False)
```

profile of v0, /device:TPU:1, one launch (start us, length us, event | category | flops | bytes accessed | tf_op | source)
XLA Modules:
  0.0 402.9 jit_solution(5441086993891481322)
XLA Ops:
  8.0 0.0 copy-start
  8.0 0.0 reduce-scatter.4.cloned.1.call-start
  8.1 0.9 copy.16
  9.0 0.1 eq.57
  9.1 0.1 eq.51
  9.2 4.5 %reduce-window.6 = s32[16,16,128]{2,1,0:T(8,128)S(1)} reduce-window(s32[16,16,128]{2,1,0:T(8,128)S(1)} %fusion.15, s32[]{:T(128)} %constant.10.clone.1), window={size=1x1x128 pad=0_0x0_0x127_0}, to_apply=%region_0.0 | reduce-window | flops 4161536 | bytes 262148 | tf_op jit(solution)/shard_map/reduce-window
  13.8 0.4 slice_reduce_fusion
  14.2 0.2 reduce-window.9
  14.4 0.1 broadcast_add_fusion
  14.5 0.1 fusion.14
  14.6 0.3 copy.18
  14.9 6.5 %eq.61 = s32[2048,16,8]{2,1,0:T(8,128)} broadcast(s32[2048,16]{1,0:T(8,128)S(1)} %copy.18), dimensions={0,1} | broadcast | bytes 1179648 | tf_op jit(solution)/shard_map/eq | solution.py:24
  21.5 0.0 copy-start.3
  21.5 11.8 %eq.62 = s32[256,8,128]{2,1,0:T(8,128)S(1)} reshape(s32[2048,16,8]{2,1,0:T(8,128)} %eq.61) | data formatting | bytes 2097152 | tf_op jit(solution)/shard_map/eq | solution.py:24
  33.2 0.0 copy-done.3
  33.3 0.1 copy.19
  33.4 0.1 eq.64
  33.5 0.7 convert_reduce_fusion
  34.2 1.5 fusion.3
  35.7 0.1 broadcast_in_dim.24
  35.8 0.0 copy-start.4
  35.8 58.5 %all_to_all.10 = bf16[64,8,1792]{2,1,0:T(8,128)(2,1)S(1)} all-to-all(bf16[64,8,1792]{2,1,0:T(8,128)(2,1)S(1)} %bitcast.34), channel_id=1, replica_groups=mesh['exp'=64,'pair'=4] {'exp'}, dimensions={0} | all-to-all | bytes 3670016 | tf_op jit(solution)/shard_map/all_to_all | solution.py:38
  94.3 0.0 copy-start.2
  94.3 1.3 copy-done.2
  95.5 0.0 copy-done.4
  95.5 2.1 fusion.9
  97.6 0.0 reduce-scatter.4.cloned.1.call-update
  97.7 0.0 reduce-scatter.6.cloned.1.call-start
  97.7 4.2 %fusion.7 = f32[512,512]{1,0:T(8,128)} fusion(bf16[1792,512]{1,0:T(8,128)(2,1)} %param.12, bf16[64,8,1792]{2,1,0:T(8,128)(2,1)} %copy-done.2), kind=kOutput, calls=%fused_computation.13 | convolution fusion | flops 939524096 | bytes 4718592 | tf_op jit(solution)/shard_map/dot_general | solution.py:41
  101.9 0.0 reduce-scatter.6.cloned.1.call-update
  102.0 0.0 all-gather.2.cloned.1.call-start
  102.0 0.5 all-gather.2.cloned.1.call-update
  102.5 16.7 %reduce-scatter.4.cloned.1.call-done = f32[128,512]{1,0:T(8,128)} async-done(((f32[512,512]{1,0:T(8,128)}), f32[128,512]{1,0:T(8,128)}) %reduce-scatter.4.cloned.1.call-update) | async-done | bytes 262160 | tf_op jit(solution)/shard_map/reduce_scatter | solution.py:43
  119.3 28.5 %reduce-scatter.6.cloned.1.call-done = f32[128,512]{1,0:T(8,128)} async-done(((f32[512,512]{1,0:T(8,128)}), f32[128,512]{1,0:T(8,128)}) %reduce-scatter.6.cloned.1.call-update) | async-done | bytes 262160 | tf_op jit(solution)/shard_map/reduce_scatter | solution.py:44
  147.8 1.1 multiply_convert_fusion
  148.9 11.0 %all_gather.6 = bf16[512,512]{1,0:T(8,128)(2,1)S(1)} all-gather(bf16[128,512]{1,0:T(8,128)(2,1)S(1)} %multiply_convert_fusion), channel_id=1, replica_groups=mesh['exp'=64,'pair'=4] {'pair'}, dimensions={0}, use_global_device_ids=true | all-gather | bytes 655360 | tf_op jit(solution)/shard_map/all_gather | solution.py:46
  159.8 0.0 copy-done
  159.8 2.4 fusion
  162.2 0.0 copy-start.1
  162.2 14.2 %all-to-all-start.1 = ((bf16[64,8,1792]{2,1,0:T(8,128)(2,1)}), bf16[64,8,1792]{2,1,0:T(8,128)(2,1)}, u32[]{:S(2)}, u32[]{:S(2)}) async-start(bf16[64,8,1792]{2,1,0:T(8,128)(2,1)} %fusion), calls=%async_computation.3 | async-start | bytes 3670016 | tf_op jit(solution)/shard_map/all_to_all | solution.py:51
  176.4 0.2 reduce-scatter.8.cloned.1.call-start
  176.7 0.1 copy.20
  176.8 0.0 copy-done.1
  176.8 0.3 fusion.4
  177.1 45.6 %all-to-all-done.1 = bf16[64,8,1792]{2,1,0:T(8,128)(2,1)} async-done(((bf16[64,8,1792]{2,1,0:T(8,128)(2,1)}), bf16[64,8,1792]{2,1,0:T(8,128)(2,1)}, u32[]{:S(2)}, u32[]{:S(2)}) %all-to-all-start.1) | async-done | bytes 1835040 | tf_op jit(solution)/shard_map/all_to_all | solution.py:51
  222.7 3.1 convolution_convert_fusion.1
  225.8 0.0 all-gather.2.cloned.1.call-done
  225.8 5.4 %fusion.2 = bf16[256,1792]{1,0:T(8,128)(2,1)S(1)} fusion(bf16[2048,1792]{1,0:T(8,128)(2,1)} %all-gather.2.cloned.1.call-done, bf16[256,1792]{1,0:T(8,128)(2,1)} %convolution_convert_fusion.1, bf16[256,2048]{1,0:T(8,128)(2,1)S(1)} %copy-done.1, f32[256]{0:T(256)S(1)} %add_rsqrt_fusion), kind=kOutput, calls=%fused_computation.6 | convolution fusion | flops 1882456064 | bytes 10224640 | tf_op jit(solution)/shard_map/dot_general | solution.py:63
  231.2 7.5 %fusion.11 = f32[2048,1792]{1,0:T(8,128)} fusion(bf16[256,1792]{1,0:T(8,128)(2,1)S(1)} %fusion.2, bf16[256,2048]{1,0:T(8,128)(2,1)S(1)} %copy-done.1, f32[256]{0:T(256)S(1)} %add_rsqrt_fusion), kind=kOutput, calls=%fused_computation.20 | convolution fusion | flops 1880621056 | bytes 16647168 | tf_op jit(solution)/shard_map/dot_general | solution.py:73
  238.7 0.0 reduce-scatter.8.cloned.1.call-update
  238.7 156.8 %reduce-scatter.8.cloned.1.call-done = f32[32,1792]{1,0:T(8,128)} async-done(((f32[2048,1792]{1,0:T(8,128)}), f32[32,1792]{1,0:T(8,128)}) %reduce-scatter.8.cloned.1.call-update) | async-done | bytes 229392 | tf_op jit(solution)/shard_map/reduce_scatter | solution.py:72
  (5 shorter events, 0.0 us)
Async XLA Ops:
  8.0 151.9 %copy-start = (bf16[512,1792]{1,0:T(8,128)(2,1)S(1)}, bf16[512,1792]{1,0:T(8,128)(2,1)}, u32[]{:S(2)}) copy-start(bf16[512,1792]{1,0:T(8,128)(2,1)} %param.13) | copy-start | bytes 5505028
  8.0 111.3 %reduce-scatter.4.cloned.1.call-start = ((), (), s32[]{:S(2)}) async-start(), calls=%async_computation.5 | async-start | bytes 1310720 | tf_op jit(solution)/shard_map/reduce_scatter | solution.py:43
  21.5 11.8 %copy-start.3 = (s32[256,8]{0,1:T(8,128)S(1)}, s32[256,8]{0,1:T(8,128)}, u32[]{:S(2)}) copy-start(s32[256,8]{0,1:T(8,128)} %param.10) | copy-start | bytes 24580
  35.8 59.8 %copy-start.4 = (bf16[1792,512]{1,0:T(8,128)(2,1)S(1)}, bf16[1792,512]{1,0:T(8,128)(2,1)}, u32[]{:S(2)}) copy-start(bf16[1792,512]{1,0:T(8,128)(2,1)} %param.11) | copy-start | bytes 5505028
  94.3 1.3 copy-start.2
  97.7 50.1 %reduce-scatter.6.cloned.1.call-start = ((), (), s32[]{:S(2)}) async-start(), calls=%async_computation.6 | async-start | bytes 1310720 | tf_op jit(solution)/shard_map/reduce_scatter | solution.py:44
  102.0 123.8 %all-gather.2.cloned.1.call-start = ((), (), s32[]{:S(2)}) async-start(), calls=%async_computation.7 | async-start | bytes 7454720 | tf_op jit(solution)/shard_map/all_gather | solution.py:65
  162.2 14.6 %copy-start.1 = (bf16[256,2048]{1,0:T(8,128)(2,1)S(1)}, bf16[256,2048]{1,0:T(8,128)(2,1)}, u32[]{:S(2)}) copy-start(bf16[256,2048]{1,0:T(8,128)(2,1)} %param.14) | copy-start | bytes 3145732
  162.2 60.5 %all-to-all-start.1 = ((bf16[64,8,1792]{2,1,0:T(8,128)(2,1)}), bf16[64,8,1792]{2,1,0:T(8,128)(2,1)}, u32[]{:S(2)}, u32[]{:S(2)}) async-start(bf16[64,8,1792]{2,1,0:T(8,128)(2,1)} %fusion), calls=%async_computation.3 | async-start | bytes 3670016 | tf_op jit(solution)/shard_map/all_to_all | solution.py:51
  176.4 219.1 %reduce-scatter.8.cloned.1.call-start = ((), (), s32[]{:S(2)}) async-start(), calls=%async_computation.8 | async-start | bytes 14909440 | tf_op jit(solution)/shard_map/reduce_scatter | solution.py:72
Sparse Core Ops, SparseCore 0:
  97.8 21.4 reduce-scatter.3
  122.0 25.7 reduce-scatter.5
Sparse Core Ops, SparseCore 1:
  105.2 84.1 all-gather.1
  238.8 156.7 reduce-scatter.7
where the time goes:
time: 407 us; the launch traced here: 403 us
  waiting for transfers between devices  248 us (61%)
  blocking collectives  69.5 us (17%)
  matrix products  26.1 us (6%)
  local copies, waits for them, and re-layouts  22 us (5%)
  between operations  15.7 us (4%)
  starting transfers between devices  14.5 us (4%)
  other arithmetic  6.95 us (2%)
    reduce_scatter x1, waiting for transfers between devices, body(): lax.psum_scatter(lax.dot_general(columns, resid, (((0,), (0,)), ((), ()))...  157 us
    all_to_all x1, blocking collectives, body(): lax.all_to_all(outgoing, 'exp', split_axis=0, concat_axis=0, tiled=True)  58.5 us
    all_to_all x1, waiting for transfers between devices, body(): lax.all_to_all(produced, 'exp', split_axis=0, concat_axis=0, tiled=True)  45.6 us
    reduce_scatter x1, waiting for transfers between devices, body(): lax.psum_scatter(up_part, 'pair', scatter_dimension=0, tiled=True)  28.5 us
    eq x4, local copies, waits for them, and re-layouts, body(): slot_of[:, :, None] == jnp.arange(slots, dtype=jnp.int32)[None, None, :]  18.4 us
    reduce_scatter x1, waiting for transfers between devices, body(): lax.psum_scatter(gate_part, 'pair', scatter_dimension=0, tiled=True)  16.7 us
    all_to_all x1, starting transfers between devices, body(): lax.all_to_all(produced, 'exp', split_axis=0, concat_axis=0, tiled=True)  14.2 us
    all_gather x1, blocking collectives, body(): lax.all_gather((jax.nn.silu(gate_pre) * up_pre).astype(jnp.bfloat16), 'pa...  11 us
  transfers between devices with their start and end apart: 5, of which 4 were waited for; matrix products, arithmetic and copies ran while one was open for 3% of the time, Pallas kernels for 0%

commit v1 on v0

v1 whole, which is shorter than its diff:
```python
import jax
import jax.numpy as jnp
from jax import lax
from jax.experimental import pallas as pl
from jax.experimental.pallas import tpu as pltpu
from jax.sharding import PartitionSpec as P

CAP = 8
MESH = pl.DeviceIdType.MESH
BF = jnp.bfloat16
F32 = jnp.float32

loss_scale = 128.0
norm_epsilon = 1e-06

W = 1792
H = 512


def dot_t(a, b):
    return lax.dot_general(a, b, (((0,), (0,)), ((), ())), preferred_element_type=F32)


def dot(a, b):
    return jnp.dot(a, b, preferred_element_type=F32)


def tiles(count, size, f, first=0):
    def step(i, carry):
        f(pl.ds(pl.multiple_of(first + i * size, 128), size))
        return carry

    lax.fori_loop(0, count, step, 0)


def kernel(
    teacher, ids, codes, student_in, proj, wg_hbm, wu_hbm, wd_hbm,
    target, grad,
    wgu, wd, weigh, packed, normed, left_x, wn, gx, rows, xk, gu, xr, act, prodf, ps, pr, vs, vr, ob, ret, tb, tg,
    wnb, pb, gxr, gs1, gr1, gs2, gr2, gt, gtt, wk, m, ms, mr, zs, zr,
    send_sem, recv_sem, local_sem,
):
    e = lax.axis_index("exp")
    x = lax.axis_index("pair")
    y, z, c = e // 16, (e // 2) % 8, e % 2
    sg = 1 - 2 * (z % 2)

    def at(dy=0, dz=0, other=False):
        yy, zz = (y + dy + 4) % 4, (z + dz + 8) % 8
        return (yy * 16 + zz * 2 + (1 - c if other else c), x)

    def at_x(dx):
        return (e, (x + dx) % 4)

    number = [0, 0]
    started = []

    def new_recv():
        number[1] += 1
        return number[1] - 1

    def copy_to(src, dst, device, recv=None):
        i = number[0]
        number[0] += 1
        copy = pltpu.make_async_remote_copy(
            src_ref=src, dst_ref=dst, send_sem=send_sem.at[i],
            recv_sem=recv_sem.at[new_recv() if recv is None else recv],
            device_id=device, device_id_type=MESH,
        )
        copy.start()
        started.append(copy)
        return copy

    def arrival(dst, recv):
        return pltpu.make_async_remote_copy(
            src_ref=dst, dst_ref=dst, send_sem=send_sem.at[0], recv_sem=recv_sem.at[recv],
            device_id=at(other=True), device_id_type=MESH,
        )

    weights = [
        pltpu.make_async_copy(wg_hbm, wgu.at[0], local_sem.at[0]),
        pltpu.make_async_copy(wu_hbm, wgu.at[1], local_sem.at[1]),
        pltpu.make_async_copy(wd_hbm, wd, local_sem.at[2]),
    ]

    barrier = pltpu.get_barrier_semaphore()
    peers = [at(dy=dy, dz=dz) for dy in range(4) for dz in (0, 1, -1, 2, -2, 3, -3) if dy or dz]
    peers += [at(dz=4), at(other=True)] + [at_x(d) for d in (1, 2, 3)]
    for peer in peers:
        pl.semaphore_signal(barrier, inc=1, device_id=peer, device_id_type=MESH)

    place = lax.broadcasted_iota(jnp.int32, (128, 256), 0)
    hop = (place >> 3) & 3
    shift = jnp.where(hop == 0, 0, jnp.where(hop == 1, -sg, jnp.where(hop == 2, sg, 2)))
    expert = ((y + 4 - (place >> 5)) & 3) * 4 + ((z // 2 + 4 + shift) & 3)
    hit = jnp.zeros((128, 256), F32)
    code = jnp.zeros((128, 256), jnp.int32)
    for k in range(8):
        same = ids[k:k + 1, :] == expert
        hit = jnp.where(same, 1.0, hit)
        code = jnp.where(same, codes[k:k + 1, :], code)
    ahead = lax.broadcasted_iota(jnp.int32, (256, 256), 0) < lax.broadcasted_iota(jnp.int32, (256, 256), 1)
    rank = dot(hit.astype(BF), jnp.where(ahead, 1.0, 0.0).astype(BF))
    chosen = jnp.where(rank == (place & 7).astype(F32), hit, 0.0)
    weigh[...] = (chosen * code.astype(F32) * (1.0 / 256.0)).astype(BF)
    chosen = chosen.astype(BF)

    def pack(cols):
        low = dot(chosen, teacher[:, cols]).reshape(16, 8, 128)
        high = dot(chosen, teacher[:, pl.ds(pl.multiple_of(896 + cols.start, 128), 128)]).reshape(16, 8, 128)
        packed[:, :, cols] = jnp.concatenate([low, high], axis=1).astype(BF)

    tiles(7, 128, pack)
    pl.semaphore_wait(barrier, len(peers))

    out_hop = (0, -1, 2, -3)
    direct, via, over, over_via = {}, {}, {}, {}
    direct[0], via[0] = new_recv(), new_recv()
    for d in (1, 3, 2):
        copy_to(packed.at[d * 4], rows.at[0, 0, 0, d], at(dy=-d), direct[0])
    for d in (0, 1, 3, 2):
        copy_to(packed.at[d * 4], rows.at[1, 0, 0, d], at(dy=-d, dz=sg), via[0])
    for j in (1, 2, 3):
        direct[j] = new_recv()
        for d in (0, 1, 3, 2):
            copy_to(packed.at[d * 4 + j], rows.at[0, j, 0, d], at(dy=-d, dz=out_hop[j] * sg), direct[j])
    rows[0, 0, 0, 0] = packed[0]
    for copy in weights:
        copy.start()

    wide = student_in[...].astype(F32)
    scale = 1.0 / jnp.sqrt(jnp.mean(wide * wide, axis=1, keepdims=True) + norm_epsilon)
    normed[...] = (wide * scale).astype(BF)
    left_x[...] = normed[:, pl.ds(pl.multiple_of(x * 512, 512), 512)].astype(F32).T.astype(BF)

    def early(cols):
        gx[:, :, :, cols] = dot(left_x[...], normed[:, cols]).reshape(8, 2, 32, 256).astype(BF)

    def early_rows(cols):
        out = dot(weigh[...], normed[:, cols]).reshape(4, 4, 8, 256)
        for j in range(4):
            wn[j, :, cols] = jnp.concatenate([out[d, j] for d in range(4)], axis=0).astype(BF)

    gram = {}

    def gram_start():
        tiles(8, 256, early)
        gram["core"] = copy_to(gx.at[:, 1 - c], gxr, at(other=True))

    def gram_0():
        gram["core"].wait_recv()
        for q in range(4):
            cols = slice(q * 512, q * 512 + 512)
            gs1[q] = (gx[:, c, :, cols].astype(F32) + gxr[:, :, cols].astype(F32)).astype(BF)
        gram["y"] = [copy_to(gs1.at[(y + d) % 4], gr1.at[d], at(dy=d)) for d in (1, 3, 2)]

    def gram_1():
        for copy in gram["y"]:
            copy.wait_recv()
        total = gs1[y].astype(F32) + sum(gr1[d].astype(F32) for d in (1, 2, 3))
        gs2[...] = total.astype(BF)
        gram["z"] = [copy_to(gs2.at[(z + d) % 8], gr2.at[d], at(dz=d)) for d in (1, 7, 2, 6, 3, 5, 4)]

    def gram_2():
        for copy in gram["z"]:
            copy.wait_recv()
        total = gs2[z].astype(F32) + sum(gr2[d].astype(F32) for d in range(1, 8))
        gt[x] = total.astype(BF)
        gram["x"] = [copy_to(gt.at[x], gt.at[x], at_x(d)) for d in (1, 3, 2)]

    early_y, early_wn = [], []

    def send_early():
        tiles(8, 256, early_rows)
        early_y.extend([copy_to(proj, pb.at[y], at(dy=d)) for d in (1, 3, 2)])
        pb[y] = proj[...]
        for j in range(4):
            early_wn.append(new_recv())
            for d in (0, 1, 3, 2):
                cols = pl.ds(pl.multiple_of(((y + 4 - d) % 4) * 512, 512), 512)
                if j == 0 and d == 0:
                    wnb[0, 0] = wn[0, :, cols]
                else:
                    copy_to(wn.at[j, :, cols], wnb.at[j, d], at(dy=-d, dz=out_hop[j] * sg), early_wn[j])

    def student():
        for copy in early_y + gram["x"]:
            copy.wait_recv()
        gtt[...] = gt[...].reshape(128, 512).astype(F32).T.astype(BF)

        def step(cols):
            m[:, :, :, cols] = dot(gtt[...], pb[:, :, cols].reshape(128, 256)).reshape(8, 2, 32, 256)

        tiles(7, 256, step)
        for j in range(4):
            into = wnb.at[j, pl.ds(1, 3)] if j == 0 else wnb.at[j]
            arrival(into, early_wn[j]).wait_recv()
            blocks = [wnb[j, d].astype(F32) for d in range(4)]
            order = [blocks[(d + 4 - g) % 4][d * 8:d * 8 + 8] for g in range(4) for d in range(4)]
            wk[j] = jnp.concatenate(order, axis=0).T.astype(BF)

    to_x, act_x, back_core, back_pair, back_z, round_y, far_y = {}, {}, {}, {}, {}, {}, {}

    def arrive(j):
        into = rows.at[0, 0, 0, pl.ds(1, 3)] if j == 0 else rows.at[0, j, 0]
        arrival(into, direct[j]).wait_recv()
        over[j] = copy_to(rows.at[0, j, 0], rows.at[0, j, 1], at(other=True))
        if j:
            via[j] = new_recv()
            copy_to(rows.at[0, j, 0], rows.at[1, j, 0], at(dz=sg), via[j])

    def arrive_via(j):
        arrival(rows.at[1, j, 0], via[j]).wait_recv()
        over_via[j] = copy_to(rows.at[1, j, 0], rows.at[1, j, 1], at(other=True))

    def gate_up(j):
        over[j].wait_recv()
        over_via[j].wait_recv()

        def unfold(cols):
            block = rows[:, j, :, :, :, cols].astype(F32).reshape(16, 2, 8, 128)
            xk[:, cols] = block[:, 0].reshape(128, 128).astype(BF)
            xk[:, pl.ds(pl.multiple_of(896 + cols.start, 128), 128)] = block[:, 1].reshape(128, 128).astype(BF)

        tiles(7, 128, unfold)
        if j == 0:
            weights[0].wait()
            weights[1].wait()
        for part in range(2):
            def step(cols):
                out = dot(xk[...], wgu[part, :, cols])
                gu[j, part, :, :, cols] = out.reshape(4, 32, 256).astype(BF)

            tiles(2, 256, step)
        to_x[j] = [copy_to(gu.at[j, :, (x + d) % 4], xr.at[j, d], at_x(d)) for d in (1, 3, 2)]

    def activate(j):
        for copy in to_x[j]:
            copy.wait_recv()
        gate, up = [
            gu[j, part, x].astype(F32) + sum(xr[j, d, part].astype(F32) for d in (1, 2, 3)) for part in range(2)
        ]
        act[j, x] = (gate / (1.0 + jnp.exp(-gate)) * up).astype(BF)
        act_x[j] = [copy_to(act.at[j, x], act.at[j, x], at_x(d)) for d in (1, 3, 2)]

    def down(j):
        for copy in act_x[j]:
            copy.wait_recv()
        if j == 0:
            weights[2].wait()

        def step(cols):
            out = dot(act[j].reshape(128, H), wd[:, cols]).reshape(4, 32, 256)
            for i in range(2):
                prodf[j, i, :, cols] = out[2 * i]
                ps[j, i, :, cols] = out[2 * i + 1].astype(BF)

        tiles(7, 256, step)
        back_core[j] = copy_to(ps.at[j], pr.at[j], at(other=True))

    def core_sum(j):
        back_core[j].wait_recv()

        def step(cols):
            vs[j, :, cols] = (prodf[j, 1, :, cols] + pr[j, 1, :, cols].astype(F32)).astype(BF)

        tiles(7, 256, step)
        back_pair[j] = copy_to(vs.at[j], vr.at[j], at(dz=sg))

    def pair_sum(j):
        back_pair[j].wait_recv()

        def step(cols):
            ob[j, 0, :, cols] = (
                prodf[j, 0, :, cols] + pr[j, 0, :, cols].astype(F32) + vr[j, :, cols].astype(F32)
            ).astype(BF)

        tiles(7, 256, step)
        round_y[j] = [copy_to(ob.at[j, 0], ob.at[j, g], at(dy=g)) for g in (1, 3)]
        if j:
            back_z[j] = copy_to(ob.at[j, 0], ret.at[j], at(dz=-j * sg))

    def relay(j):
        low, high = pl.ds(0, 16), pl.ds(16, 16)
        round_y[j][0].wait_recv()
        far_y[j] = [copy_to(ob.at[j, 1, low], ob.at[j, 2, low], at(dy=1))]
        round_y[j][1].wait_recv()
        far_y[j].append(copy_to(ob.at[j, 3, high], ob.at[j, 2, high], at(dy=-1)))

    def teacher_part(j):
        for copy in far_y[j]:
            copy.wait_recv()

        def step(cols):
            part = dot(wk[j], ob[j, :, :, cols].reshape(128, 256))
            m[:, :, :, cols] -= part.reshape(8, 2, 32, 256)

        tiles(7, 256, step)

    stages = (arrive, arrive_via, gate_up, activate, down, core_sum, pair_sum, relay)
    after = {0: gram_start, 1: send_early, 2: gram_0, 4: gram_1, 5: gram_2, 7: student}
    for t in range(len(stages) + 3):
        for j in range(4):
            if 0 <= t - j < len(stages):
                stages[t - j](j)
        if t in after:
            after[t]()
        if t >= 8:
            teacher_part(t - 8)

    parts = ((0, 4), (1024, 3))
    over_m = []
    for copy in far_y[3]:
        copy.wait_recv()

    def finish(cols):
        part = dot(wk[3], ob[3, :, :, cols].reshape(128, 256))
        m[:, :, :, cols] -= part.reshape(8, 2, 32, 256)
        ms[:, :, cols] = m[:, 1 - c, :, cols].astype(BF)

    for first, count in parts:
        tiles(count, 256, finish, first)
        span = pl.ds(first, count * 256)
        over_m.append(copy_to(ms.at[:, :, span], mr.at[:, :, span], at(other=True)))

    for j in (1, 2, 3):
        back_z[j].wait_recv()

    def sort_rows(cols):
        blocks = [ob[0, 0, :, cols].astype(F32)] + [ret[j, :, cols].astype(F32) for j in (1, 2, 3)]
        for d in range(4):
            tb[d, :, cols] = jnp.concatenate([b[d * 8:d * 8 + 8] for b in blocks], axis=0).astype(BF)

    tiles(7, 256, sort_rows)
    to_owner = [copy_to(tb.at[d], tg.at[d], at(dy=d)) for d in (1, 3, 2)]
    tg[0] = tb[0]

    def mine(d, first, count, cols):
        zz = (z + 8 + d) % 8
        span = slice(first, first + count)
        return m[zz, c, span, cols] + mr[zz, span, cols].astype(F32)

    hops = {}
    for step in range(4):
        for half, (start, count) in enumerate(parts):
            cols = pl.ds(start, count * 256)
            if step == 0:
                over_m[half].wait_recv()
            for way, sign in ((0, -1), (1, 1)):
                slot = step * 2 + way
                far = sign * (4 - step)
                if step == 0:
                    zs[slot, 0:16, cols] = mine(far, 16 * way, 16, cols).astype(BF)
                    src, dst = zs.at[slot, pl.ds(0, 16), cols], zr.at[slot, pl.ds(0, 16), cols]
                else:
                    hops[step - 1, half, way].wait_recv()
                    if step == 1:
                        first = 16 * way
                        total = mine(far, first, 16, cols) + zr[slot - 2, 0:16, cols].astype(F32)
                        zs[slot, first:first + 16, cols] = total.astype(BF)
                        zs[slot, 16 - first:32 - first, cols] = mine(far, 16 - first, 16, cols).astype(BF)
                    else:
                        zs[slot, :, cols] = (mine(far, 0, 32, cols) + zr[slot - 2, :, cols].astype(F32)).astype(BF)
                    src, dst = zs.at[slot, :, cols], zr.at[slot, :, cols]
                hops[step, half, way] = copy_to(src, dst, at(dz=sign))
        if step == 1:
            for copy in to_owner:
                copy.wait_recv()

            def write_target(cols):
                target[:, cols] = dot_t(weigh[...], tg[:, :, cols].reshape(128, 256)).astype(BF)

            tiles(7, 256, write_target)
    for half, (start, count) in enumerate(parts):
        cols = pl.ds(start, count * 256)
        total = mine(0, 0, 32, cols)
        for way in range(2):
            hops[3, half, way].wait_recv()
            total += zr[6 + way, :, cols].astype(F32)
        grad[:, cols] = total * (loss_scale / 16384)
    for copy in started:
        copy.wait_send()


N_COPIES = 19 + 3 + 8 + 12 + 12 + 4 + 4 + 3 + 16 + 3 + 15 + 14 + 3 + 2 + 16


def body(teacher_in, expert_ids, gate_codes, w_gate, w_up, w_down, student_in, projection):
    vmem = pl.BlockSpec(memory_space=pltpu.VMEM)
    hbm = pl.BlockSpec(memory_space=pl.ANY)
    return pl.pallas_call(
        kernel,
        out_shape=(
            jax.ShapeDtypeStruct((256, W), BF),
            jax.ShapeDtypeStruct((32, W), F32),
        ),
        in_specs=[vmem] * 5 + [hbm] * 3,
        out_specs=(vmem, vmem),
        scratch_shapes=[
            pltpu.VMEM((2, W, H), BF),
            pltpu.VMEM((H, W), BF),
            pltpu.VMEM((128, 256), BF),
            pltpu.VMEM((16, 16, W // 2), BF),
            pltpu.VMEM((256, 2048), BF),
            pltpu.VMEM((512, 256), BF),
            pltpu.VMEM((4, 32, 2048), BF),
            pltpu.VMEM((8, 2, 32, 2048), BF),
            pltpu.VMEM((2, 4, 2, 4, 16, W // 2), BF),
            pltpu.VMEM((128, W), BF),
            pltpu.VMEM((4, 2, 4, 32, H), BF),
            pltpu.VMEM((4, 4, 2, 32, H), BF),
            pltpu.VMEM((4, 4, 32, H), BF),
            pltpu.VMEM((4, 2, 32, W), F32),
            pltpu.VMEM((4, 2, 32, W), BF),
            pltpu.VMEM((4, 2, 32, W), BF),
            pltpu.VMEM((4, 32, W), BF),
            pltpu.VMEM((4, 32, W), BF),
            pltpu.VMEM((4, 4, 32, W), BF),
            pltpu.VMEM((4, 32, W), BF),
            pltpu.VMEM((4, 32, W), BF),
            pltpu.VMEM((4, 32, W), BF),
            pltpu.VMEM((4, 4, 32, 512), BF),
            pltpu.VMEM((4, 32, W), BF),
            pltpu.VMEM((8, 32, 2048), BF),
            pltpu.VMEM((4, 8, 32, 512), BF),
            pltpu.VMEM((4, 8, 32, 512), BF),
            pltpu.VMEM((8, 32, 512), BF),
            pltpu.VMEM((8, 32, 512), BF),
            pltpu.VMEM((4, 32, 512), BF),
            pltpu.VMEM((512, 128), BF),
            pltpu.VMEM((4, 512, 128), BF),
            pltpu.VMEM((8, 2, 32, W), F32),
            pltpu.VMEM((8, 32, W), BF),
            pltpu.VMEM((8, 32, W), BF),
            pltpu.VMEM((8, 32, W), BF),
            pltpu.VMEM((8, 32, W), BF),
            pltpu.SemaphoreType.DMA((N_COPIES,)),
            pltpu.SemaphoreType.DMA((N_COPIES,)),
            pltpu.SemaphoreType.DMA((3,)),
        ],
        compiler_params=pltpu.CompilerParams(
            collective_id=0, has_side_effects=True, vmem_limit_bytes=52 * 1024 * 1024
        ),
        cost_estimate=pl.CostEstimate(flops=8_000_000_000, bytes_accessed=12_000_000, transcendentals=0),
    )(teacher_in, expert_ids.T, gate_codes.T, student_in, projection, w_gate, w_up, w_down)


def solution(mesh):
    in_specs = (
        P("exp", "pair"),
        P("exp", None),
        P("exp", None),
        P("pair", "exp"),
        P("pair", "exp"),
        P("exp", "pair"),
        P("exp", None),
        P("exp", "pair"),
    )
    out_specs = (P("exp", "pair"), P("exp", "pair"))
    return jax.shard_map(body, mesh=mesh, in_specs=in_specs, out_specs=out_specs, check_vma=False)
```

time: 407 us -> 102 us (0.25)
  waiting for transfers between devices: 248 us -> 0 us
  Pallas kernels: 0 us -> 96.5 us
  blocking collectives: 69.5 us -> 0 us
  matrix products: 26.1 us -> 0 us
  local copies, waits for them, and re-layouts: 22 us -> 3.9 us
  between operations: 15.7 us -> 0.65 us
  starting transfers between devices: 14.5 us -> 0 us
  other arithmetic: 6.95 us -> 0 us
    reduce_scatter x3 -> x0, waiting for transfers between devices: 202 us -> none  [the longest x1 157 us: body(): lax.psum_scatter(lax.dot_general(columns, resid, (((0,), (0,)), ((), ()))...]
    pallas_call x0 -> x1, Pallas kernels: none -> 96.5 us  [body(): pl.pallas_call(kernel, out_shape=(jax.ShapeDtypeStruct((256, W), BF), jax...]
    all_to_all x1 -> x0, blocking collectives: 58.5 us -> none  [body(): lax.all_to_all(outgoing, 'exp', split_axis=0, concat_axis=0, tiled=True)]
    all_to_all x1 -> x0, waiting for transfers between devices: 45.6 us -> none  [body(): lax.all_to_all(produced, 'exp', split_axis=0, concat_axis=0, tiled=True)]
    dot_general x7 -> x0, matrix products: 26.1 us -> none  [the longest x1 7.49 us: body(): lax.dot_general(columns, resid, (((0,), (0,)), ((), ())), preferred_eleme...]
    eq x6 -> x0, local copies, waits for them, and re-layouts: 18.6 us -> none  [the longest x4 18.4 us: body(): slot_of[:, :, None] == jnp.arange(slots, dtype=jnp.int32)[None, None, :]]
    all_to_all x1 -> x0, starting transfers between devices: 14.2 us -> none  [body(): lax.all_to_all(produced, 'exp', split_axis=0, concat_axis=0, tiled=True)]
    all_gather x1 -> x0, blocking collectives: 11 us -> none  [body(): lax.all_gather((jax.nn.silu(gate_pre) * up_pre).astype(jnp.bfloat16), 'pa...]
  transfers between devices with their start and end apart: 5 -> 0, of which waited for: 4 -> 0; matrix products, arithmetic and copies ran while one was open for 3% -> 0% of each run, Pallas kernels for 0% -> 0%
where the time goes in v1:
time: 102 us; the launch traced here: 101 us
  Pallas kernels  96.5 us (95%)
  local copies, waits for them, and re-layouts  3.9 us (4%)
    pallas_call x1, Pallas kernels, body(): pl.pallas_call(kernel, out_shape=(jax.ShapeDtypeStruct((256, W), BF), jax...  96.5 us
    unnamed x8, local copies, waits for them, and re-layouts  3.9 us

profile of v1, /device:TPU:1, one launch (start us, length us, event | category | flops | bytes accessed | tf_op | source)
XLA Modules:
  0.0 101.1 jit_solution(5628874461339756121)
XLA Ops:
  0.6 0.0 copy-start
  0.6 0.9 copy-done
  1.5 0.0 copy-start.1
  1.5 0.7 copy-done.1
  2.2 0.0 copy-start.2
  2.2 0.7 copy-done.2
  2.9 96.5 %shard_map.95 = (bf16[256,1792]{1,0:T(8,128)(2,1)S(1)}, f32[32,1792]{1,0:T(8,128)S(1)}) custom-call(bf16[256,1792]{1,0:T(8,128)(2,1)} %teacher.1, s32[8,256]{1,0:T(8,128)S(1)} %bitcast.2, s32[8,256]{1,0:T(8,128)S(1)} %bitcast.3, bf16[256,2048]{1,0:T(8,128)(2,1)} %student_in.1, bf16[32,1792]{1,0:T(8,128)(2,1)S(1)} %copy-done, bf16[1792,512]{1,0:T(8,128)(2,1)} %wg_hbm.1, ...), custom_call_target="tpu_custom_call" | custom-call | flops 8000000000 | bytes 12000000 | tf_op jit(solution)/shard_map/pallas_call | solution.py:391
  99.5 0.9 copy.12
  100.4 0.7 copy.13
Async XLA Ops:
  0.6 0.9 copy-start
  1.5 0.7 copy-start.1
  2.2 0.7 copy-start.2

commit v2 on v1

--- a/solution.py
+++ b/solution.py
@@ -34,10 +34,10 @@
 
 
 def kernel(
-    teacher, ids, codes, student_in, proj, wg_hbm, wu_hbm, wd_hbm,
-    target, grad,
-    wgu, wd, weigh, packed, normed, left_x, wn, gx, rows, xk, gu, xr, act, prodf, ps, pr, vs, vr, ob, ret, tb, tg,
-    wnb, pb, gxr, gs1, gr1, gs2, gr2, gt, gtt, wk, m, ms, mr, zs, zr,
+    ids_hbm, codes_hbm, proj_hbm, teacher_hbm, student_hbm, wg_hbm, wu_hbm, wd_hbm,
+    target_hbm, grad_hbm, target, grad, tg, ids, codes, proj, teacher, student_in,
+    wgu, wd, weigh, packed, normed, left_x, wn, gx, rows, xk, gu, xr, act, prodf, ps, pr, vs, vr, ob, ret, tb,
+    wnb, pb, gxr, gs1, gr1, gs2, gr2, gt, gtt, gtf, wkt, wk, m, zs, zr,
     send_sem, recv_sem, local_sem,
 ):
     e = lax.axis_index("exp")
@@ -82,6 +82,14 @@
         pltpu.make_async_copy(wu_hbm, wgu.at[1], local_sem.at[1]),
         pltpu.make_async_copy(wd_hbm, wd, local_sem.at[2]),
     ]
+    operands = [
+        pltpu.make_async_copy(src, dst, local_sem.at[3 + i])
+        for i, (src, dst) in enumerate((
+            (ids_hbm, ids), (codes_hbm, codes), (teacher_hbm, teacher), (student_hbm, student_in), (proj_hbm, proj),
+        ))
+    ]
+    for copy in operands:
+        copy.start()
 
     barrier = pltpu.get_barrier_semaphore()
     peers = [at(dy=dy, dz=dz) for dy in range(4) for dz in (0, 1, -1, 2, -2, 3, -3) if dy or dz]
@@ -89,6 +97,8 @@
     for peer in peers:
         pl.semaphore_signal(barrier, inc=1, device_id=peer, device_id_type=MESH)
 
+    operands[0].wait()
+    operands[1].wait()
     place = lax.broadcasted_iota(jnp.int32, (128, 256), 0)
     hop = (place >> 3) & 3
     shift = jnp.where(hop == 0, 0, jnp.where(hop == 1, -sg, jnp.where(hop == 2, sg, 2)))
@@ -110,24 +120,26 @@
         high = dot(chosen, teacher[:, pl.ds(pl.multiple_of(896 + cols.start, 128), 128)]).reshape(16, 8, 128)
         packed[:, :, cols] = jnp.concatenate([low, high], axis=1).astype(BF)
 
+    operands[2].wait()
     tiles(7, 128, pack)
     pl.semaphore_wait(barrier, len(peers))
 
     out_hop = (0, -1, 2, -3)
     direct, via, over, over_via = {}, {}, {}, {}
-    direct[0], via[0] = new_recv(), new_recv()
-    for d in (1, 3, 2):
-        copy_to(packed.at[d * 4], rows.at[0, 0, 0, d], at(dy=-d), direct[0])
-    for d in (0, 1, 3, 2):
-        copy_to(packed.at[d * 4], rows.at[1, 0, 0, d], at(dy=-d, dz=sg), via[0])
-    for j in (1, 2, 3):
+    for j in range(4):
         direct[j] = new_recv()
-        for d in (0, 1, 3, 2):
-            copy_to(packed.at[d * 4 + j], rows.at[0, j, 0, d], at(dy=-d, dz=out_hop[j] * sg), direct[j])
+        for d in (1, 3, 2, 0):
+            if j or d:
+                copy_to(packed.at[d * 4 + j], rows.at[0, j, 0, d], at(dy=-d, dz=out_hop[j] * sg), direct[j])
+        if j == 0:
+            via[0] = new_recv()
+            for d in (0, 1, 3, 2):
+                copy_to(packed.at[d * 4], rows.at[1, 0, 0, d], at(dy=-d, dz=sg), via[0])
     rows[0, 0, 0, 0] = packed[0]
     for copy in weights:
         copy.start()
 
+    operands[3].wait()
     wide = student_in[...].astype(F32)
     scale = 1.0 / jnp.sqrt(jnp.mean(wide * wide, axis=1, keepdims=True) + norm_epsilon)
     normed[...] = (wide * scale).astype(BF)
@@ -168,46 +180,64 @@
         gt[x] = total.astype(BF)
         gram["x"] = [copy_to(gt.at[x], gt.at[x], at_x(d)) for d in (1, 3, 2)]
 
-    early_y, early_wn = [], []
-
-    def send_early():
+    early_y, swap = [], []
+
+    def send_proj():
+        operands[4].wait()
+        early_y.extend([copy_to(proj, pb.at[0, y], at(dy=d)) for d in (1, 3, 2)])
+        pb[0, y] = proj[...]
+
+    def wn_rows():
         tiles(8, 256, early_rows)
-        early_y.extend([copy_to(proj, pb.at[y], at(dy=d)) for d in (1, 3, 2)])
-        pb[y] = proj[...]
-        for j in range(4):
-            early_wn.append(new_recv())
-            for d in (0, 1, 3, 2):
-                cols = pl.ds(pl.multiple_of(((y + 4 - d) % 4) * 512, 512), 512)
-                if j == 0 and d == 0:
-                    wnb[0, 0] = wn[0, :, cols]
-                else:
-                    copy_to(wn.at[j, :, cols], wnb.at[j, d], at(dy=-d, dz=out_hop[j] * sg), early_wn[j])
-
-    def student():
-        for copy in early_y + gram["x"]:
-            copy.wait_recv()
-        gtt[...] = gt[...].reshape(128, 512).astype(F32).T.astype(BF)
-
-        def step(cols):
-            m[:, :, :, cols] = dot(gtt[...], pb[:, :, cols].reshape(128, 256)).reshape(8, 2, 32, 256)
-
-        tiles(7, 256, step)
+
+    early_wn = {}
+
+    def wn_send(j):
+        early_wn[j] = new_recv()
+        for d in (0, 1, 3, 2):
+            cols = pl.ds(pl.multiple_of(((y + 4 - d) % 4) * 512, 512), 512)
+            if j == 0 and d == 0:
+                wnb[0, 0] = wn[0, :, cols]
+            else:
+                copy_to(wn.at[j, :, cols], wnb.at[j, d], at(dy=-d, dz=out_hop[j] * sg), early_wn[j])
+
+    def swap_proj():
+        for copy in early_y:
+            copy.wait_recv()
+        swap.append(copy_to(pb.at[0], pb.at[1], at(other=True)))
+
+    other_k = pl.ds(128, 128)
+
+    def student_rows():
         for j in range(4):
             into = wnb.at[j, pl.ds(1, 3)] if j == 0 else wnb.at[j]
             arrival(into, early_wn[j]).wait_recv()
             blocks = [wnb[j, d].astype(F32) for d in range(4)]
             order = [blocks[(d + 4 - g) % 4][d * 8:d * 8 + 8] for g in range(4) for d in range(4)]
-            wk[j] = jnp.concatenate(order, axis=0).T.astype(BF)
-
-    to_x, act_x, back_core, back_pair, back_z, round_y, far_y = {}, {}, {}, {}, {}, {}, {}
+            wkt[j] = jnp.concatenate(order, axis=0).T.reshape(8, 2, 32, 128).astype(BF)
+            wk[j, :, :, 0:128] = wkt[j, :, c]
+        swap.append(copy_to(wkt.at[:, :, 1 - c], wk.at[:, :, :, other_k], at(other=True)))
+
+    def gram_3():
+        for copy in gram["x"]:
+            copy.wait_recv()
+        gtt[...] = gt[...].reshape(128, 512).astype(F32).T.reshape(8, 2, 32, 128).astype(BF)
+        gtf[:, :, 0:128] = gtt[:, c]
+        swap.append(copy_to(gtt.at[:, 1 - c], gtf.at[:, :, other_k], at(other=True)))
+
+    to_x, act_x, back_core, back_pair, back_z, round_y, far_y, whole = {}, {}, {}, {}, {}, {}, {}, {}
+    parts = ((0, 4), (1024, 3))
+
+    def spans(j):
+        return parts if j == 3 else ((0, 7),)
 
     def arrive(j):
         into = rows.at[0, 0, 0, pl.ds(1, 3)] if j == 0 else rows.at[0, j, 0]
         arrival(into, direct[j]).wait_recv()
-        over[j] = copy_to(rows.at[0, j, 0], rows.at[0, j, 1], at(other=True))
         if j:
             via[j] = new_recv()
             copy_to(rows.at[0, j, 0], rows.at[1, j, 0], at(dz=sg), via[j])
+        over[j] = copy_to(rows.at[0, j, 0], rows.at[0, j, 1], at(other=True))
 
     def arrive_via(j):
         arrival(rows.at[1, j, 0], via[j]).wait_recv()
@@ -255,97 +285,121 @@
                 prodf[j, i, :, cols] = out[2 * i]
                 ps[j, i, :, cols] = out[2 * i + 1].astype(BF)
 
-        tiles(7, 256, step)
-        back_core[j] = copy_to(ps.at[j], pr.at[j], at(other=True))
+        for first, count in spans(j):
+            tiles(count, 256, step, first)
+            cols = pl.ds(first, count * 256)
+            back_core[j, first] = copy_to(ps.at[j, :, :, cols], pr.at[j, :, :, cols], at(other=True))
 
     def core_sum(j):
-        back_core[j].wait_recv()
-
         def step(cols):
             vs[j, :, cols] = (prodf[j, 1, :, cols] + pr[j, 1, :, cols].astype(F32)).astype(BF)
 
-        tiles(7, 256, step)
-        back_pair[j] = copy_to(vs.at[j], vr.at[j], at(dz=sg))
+        for first, count in spans(j):
+            back_core[j, first].wait_recv()
+            tiles(count, 256, step, first)
+            cols = pl.ds(first, count * 256)
+            back_pair[j, first] = copy_to(vs.at[j, :, cols], vr.at[j, :, cols], at(dz=sg))
 
     def pair_sum(j):
-        back_pair[j].wait_recv()
-
         def step(cols):
-            ob[j, 0, :, cols] = (
+            ob[j, 0, 0, :, cols] = (
                 prodf[j, 0, :, cols] + pr[j, 0, :, cols].astype(F32) + vr[j, :, cols].astype(F32)
             ).astype(BF)
 
-        tiles(7, 256, step)
-        round_y[j] = [copy_to(ob.at[j, 0], ob.at[j, g], at(dy=g)) for g in (1, 3)]
+        for first, count in spans(j):
+            back_pair[j, first].wait_recv()
+            tiles(count, 256, step, first)
+            cols = pl.ds(first, count * 256)
+            round_y[j, first] = [
+                copy_to(ob.at[j, 0, 0, :, cols], ob.at[j, 0, g, :, cols], at(dy=g)) for g in (1, 3)
+            ]
         if j:
-            back_z[j] = copy_to(ob.at[j, 0], ret.at[j], at(dz=-j * sg))
+            back_z[j] = copy_to(ob.at[j, 0, 0], ret.at[j], at(dz=-j * sg))
 
     def relay(j):
         low, high = pl.ds(0, 16), pl.ds(16, 16)
-        round_y[j][0].wait_recv()
-        far_y[j] = [copy_to(ob.at[j, 1, low], ob.at[j, 2, low], at(dy=1))]
-        round_y[j][1].wait_recv()
-        far_y[j].append(copy_to(ob.at[j, 3, high], ob.at[j, 2, high], at(dy=-1)))
-
-    def teacher_part(j):
-        for copy in far_y[j]:
-            copy.wait_recv()
+        for first, count in spans(j):
+            cols = pl.ds(first, count * 256)
+            far_y[j, first] = []
+            for side, (g, rows_g, dy) in enumerate(((1, low, 1), (3, high, -1))):
+                round_y[j, first][side].wait_recv()
+                far_y[j, first].append(
+                    copy_to(ob.at[j, 0, g, rows_g, cols], ob.at[j, 0, 2, rows_g, cols], at(dy=dy))
+                )
+
+    def far(j):
+        for first, count in spans(j):
+            for copy in far_y[j, first]:
+                copy.wait_recv()
+            cols = pl.ds(first, count * 256)
+            whole[j, first] = copy_to(ob.at[j, 0, :, :, cols], ob.at[j, 1, :, :, cols], at(other=True))
+
+    def product(j, cols):
+        return dot(wk[j].reshape(256, 256), ob[j, :, :, :, cols].reshape(256, 256))
+
+    def student():
+        for copy in swap:
+            copy.wait_recv()
+        for j in range(3):
+            whole[j, 0].wait_recv()
 
         def step(cols):
-            part = dot(wk[j], ob[j, :, :, cols].reshape(128, 256))
-            m[:, :, :, cols] -= part.reshape(8, 2, 32, 256)
+            part = dot(gtf[...].reshape(256, 256), pb[:, :, :, cols].reshape(256, 256))
+            part -= product(0, cols) + product(1, cols) + product(2, cols)
+            m[:, :, cols] = part.reshape(8, 32, 256)
 
         tiles(7, 256, step)
 
-    stages = (arrive, arrive_via, gate_up, activate, down, core_sum, pair_sum, relay)
-    after = {0: gram_start, 1: send_early, 2: gram_0, 4: gram_1, 5: gram_2, 7: student}
-    for t in range(len(stages) + 3):
-        for j in range(4):
-            if 0 <= t - j < len(stages):
-                stages[t - j](j)
-        if t in after:
-            after[t]()
-        if t >= 8:
-            teacher_part(t - 8)
-
-    parts = ((0, 4), (1024, 3))
-    over_m = []
-    for copy in far_y[3]:
-        copy.wait_recv()
-
-    def finish(cols):
-        part = dot(wk[3], ob[3, :, :, cols].reshape(128, 256))
-        m[:, :, :, cols] -= part.reshape(8, 2, 32, 256)
-        ms[:, :, cols] = m[:, 1 - c, :, cols].astype(BF)
-
-    for first, count in parts:
-        tiles(count, 256, finish, first)
-        span = pl.ds(first, count * 256)
-        over_m.append(copy_to(ms.at[:, :, span], mr.at[:, :, span], at(other=True)))
-
-    for j in (1, 2, 3):
-        back_z[j].wait_recv()
-
-    def sort_rows(cols):
-        blocks = [ob[0, 0, :, cols].astype(F32)] + [ret[j, :, cols].astype(F32) for j in (1, 2, 3)]
-        for d in range(4):
-            tb[d, :, cols] = jnp.concatenate([b[d * 8:d * 8 + 8] for b in blocks], axis=0).astype(BF)
-
-    tiles(7, 256, sort_rows)
-    to_owner = [copy_to(tb.at[d], tg.at[d], at(dy=d)) for d in (1, 3, 2)]
-    tg[0] = tb[0]
+    def finish(part):
+        first, count = parts[part]
+        whole[3, first].wait_recv()
+
+        def step(cols):
+            m[:, :, cols] -= product(3, cols).reshape(8, 32, 256)
+
+        tiles(count, 256, step, first)
+
+    def run(steps):
+        for name, j in steps:
+            name(j)
+
+    def when(f):
+        return (lambda _: f(), 0)
+
+    run([
+        when(wn_rows), (arrive, 0), (arrive_via, 0), when(gram_start), (arrive, 1), (arrive, 2), when(send_proj),
+        (wn_send, 3), (gate_up, 0), (arrive_via, 1), (wn_send, 1), (arrive, 3), (wn_send, 2), (gate_up, 1),
+        (arrive_via, 2), (activate, 0), when(gram_0), (gate_up, 2), (arrive_via, 3), (activate, 1), (down, 0),
+        (gate_up, 3), (core_sum, 0), (activate, 2), (down, 1), (wn_send, 0), (core_sum, 1), (activate, 3),
+        (pair_sum, 0), (down, 2), (core_sum, 2), (pair_sum, 1), (down, 3), (relay, 0), (core_sum, 3), when(gram_1),
+        (pair_sum, 2), when(student_rows), (far, 0), when(swap_proj), (pair_sum, 3), (relay, 2), (relay, 1),
+        (relay, 3), when(gram_2), (far, 2), (far, 1), when(gram_3), (far, 3), when(student),
+    ])
+
+    to_owner = []
+
+    def send_target():
+        for j in (1, 2, 3):
+            back_z[j].wait_recv()
+
+        def sort_rows(cols):
+            blocks = [ob[0, 0, 0, :, cols].astype(F32)] + [ret[j, :, cols].astype(F32) for j in (1, 2, 3)]
+            for d in range(4):
+                tb[d, :, cols] = jnp.concatenate([b[d * 8:d * 8 + 8] for b in blocks], axis=0).astype(BF)
+
+        tiles(7, 256, sort_rows)
+        to_owner.extend([copy_to(tb.at[d], tg.at[d], at(dy=d)) for d in (1, 3, 2)])
+        tg[0] = tb[0]
 
     def mine(d, first, count, cols):
-        zz = (z + 8 + d) % 8
-        span = slice(first, first + count)
-        return m[zz, c, span, cols] + mr[zz, span, cols].astype(F32)
+        return m[(z + 8 + d) % 8, first:first + count, cols]
 
     hops = {}
     for step in range(4):
         for half, (start, count) in enumerate(parts):
             cols = pl.ds(start, count * 256)
             if step == 0:
-                over_m[half].wait_recv()
+                finish(half)
             for way, sign in ((0, -1), (1, 1)):
                 slot = step * 2 + way
                 far = sign * (4 - step)
@@ -363,7 +417,13 @@
                         zs[slot, :, cols] = (mine(far, 0, 32, cols) + zr[slot - 2, :, cols].astype(F32)).astype(BF)
                     src, dst = zs.at[slot, :, cols], zr.at[slot, :, cols]
                 hops[step, half, way] = copy_to(src, dst, at(dz=sign))
+        if step == 0:
+            send_target()
         if step == 1:
+            for copy in started[:-8]:
+                copy.wait_send()
+            del started[:-8]
+        if step == 2:
             for copy in to_owner:
                 copy.wait_recv()
 
@@ -371,6 +431,8 @@
                 target[:, cols] = dot_t(weigh[...], tg[:, :, cols].reshape(128, 256)).astype(BF)
 
             tiles(7, 256, write_target)
+            target_out = pltpu.make_async_copy(target, target_hbm, local_sem.at[8])
+            target_out.start()
     for half, (start, count) in enumerate(parts):
         cols = pl.ds(start, count * 256)
         total = mine(0, 0, 32, cols)
@@ -378,15 +440,18 @@
             hops[3, half, way].wait_recv()
             total += zr[6 + way, :, cols].astype(F32)
         grad[:, cols] = total * (loss_scale / 16384)
+    grad_out = pltpu.make_async_copy(grad, grad_hbm, local_sem.at[9])
+    grad_out.start()
     for copy in started:
         copy.wait_send()
-
-
-N_COPIES = 19 + 3 + 8 + 12 + 12 + 4 + 4 + 3 + 16 + 3 + 15 + 14 + 3 + 2 + 16
+    target_out.wait()
+    grad_out.wait()
+
+
+N_COPIES = 19 + 3 + 8 + 12 + 12 + 5 + 5 + 3 + 40 + 3 + 15 + 14 + 3 + 3 + 16
 
 
 def body(teacher_in, expert_ids, gate_codes, w_gate, w_up, w_down, student_in, projection):
-    vmem = pl.BlockSpec(memory_space=pltpu.VMEM)
     hbm = pl.BlockSpec(memory_space=pl.ANY)
     return pl.pallas_call(
         kernel,
@@ -394,9 +459,17 @@
             jax.ShapeDtypeStruct((256, W), BF),
             jax.ShapeDtypeStruct((32, W), F32),
         ),
-        in_specs=[vmem] * 5 + [hbm] * 3,
-        out_specs=(vmem, vmem),
+        in_specs=[hbm] * 8,
+        out_specs=(hbm, hbm),
         scratch_shapes=[
+            pltpu.VMEM((256, W), BF),
+            pltpu.VMEM((32, W), F32),
+            pltpu.VMEM((4, 32, W), BF),
+            pltpu.VMEM((8, 256), jnp.int32),
+            pltpu.VMEM((8, 256), jnp.int32),
+            pltpu.VMEM((32, W), BF),
+            pltpu.VMEM((256, W), BF),
+            pltpu.VMEM((256, 2048), BF),
             pltpu.VMEM((2, W, H), BF),
             pltpu.VMEM((H, W), BF),
             pltpu.VMEM((128, 256), BF),
@@ -415,34 +488,33 @@
             pltpu.VMEM((4, 2, 32, W), BF),
             pltpu.VMEM((4, 32, W), BF),
             pltpu.VMEM((4, 32, W), BF),
-            pltpu.VMEM((4, 4, 32, W), BF),
-            pltpu.VMEM((4, 32, W), BF),
+            pltpu.VMEM((4, 2, 4, 32, W), BF),
             pltpu.VMEM((4, 32, W), BF),
             pltpu.VMEM((4, 32, W), BF),
             pltpu.VMEM((4, 4, 32, 512), BF),
-            pltpu.VMEM((4, 32, W), BF),
+            pltpu.VMEM((2, 4, 32, W), BF),
             pltpu.VMEM((8, 32, 2048), BF),
             pltpu.VMEM((4, 8, 32, 512), BF),
             pltpu.VMEM((4, 8, 32, 512), BF),
             pltpu.VMEM((8, 32, 512), BF),
             pltpu.VMEM((8, 32, 512), BF),
             pltpu.VMEM((4, 32, 512), BF),
-            pltpu.VMEM((512, 128), BF),
-            pltpu.VMEM((4, 512, 128), BF),
-            pltpu.VMEM((8, 2, 32, W), F32),
-            pltpu.VMEM((8, 32, W), BF),
-            pltpu.VMEM((8, 32, W), BF),
+            pltpu.VMEM((8, 2, 32, 128), BF),
+            pltpu.VMEM((8, 32, 256), BF),
+            pltpu.VMEM((4, 8, 2, 32, 128), BF),
+            pltpu.VMEM((4, 8, 32, 256), BF),
+            pltpu.VMEM((8, 32, W), F32),
             pltpu.VMEM((8, 32, W), BF),
             pltpu.VMEM((8, 32, W), BF),
             pltpu.SemaphoreType.DMA((N_COPIES,)),
             pltpu.SemaphoreType.DMA((N_COPIES,)),
-            pltpu.SemaphoreType.DMA((3,)),
+            pltpu.SemaphoreType.DMA((10,)),
         ],
         compiler_params=pltpu.CompilerParams(
-            collective_id=0, has_side_effects=True, vmem_limit_bytes=52 * 1024 * 1024
+            collective_id=0, has_side_effects=True, vmem_limit_bytes=60 * 1024 * 1024
         ),
         cost_estimate=pl.CostEstimate(flops=8_000_000_000, bytes_accessed=12_000_000, transcendentals=0),
-    )(teacher_in, expert_ids.T, gate_codes.T, student_in, projection, w_gate, w_up, w_down)
+    )(expert_ids.T, gate_codes.T, projection, teacher_in, student_in, w_gate, w_up, w_down)
 
 
 def solution(mesh):

time: 102 us -> 98.4 us (0.965)
  Pallas kernels: 96.5 us -> 94.7 us
    pallas_call x1, Pallas kernels: 96.5 us -> 94.7 us  [body(): pl.pallas_call(kernel, out_shape=(jax.ShapeDtypeStruct((256, W), BF), jax...]
    unnamed x8 -> x4, local copies, waits for them, and re-layouts: 3.9 us -> 2.89 us
where the time goes in v2:
time: 98.4 us; the launch traced here: 98.2 us
  Pallas kernels  94.7 us (96%)
  local copies, waits for them, and re-layouts  2.89 us (3%)
    pallas_call x1, Pallas kernels, body(): pl.pallas_call(kernel, out_shape=(jax.ShapeDtypeStruct((256, W), BF), jax...  94.7 us
    unnamed x4, local copies, waits for them, and re-layouts  2.89 us

profile of v2, /device:TPU:1, one launch (start us, length us, event | category | flops | bytes accessed | tf_op | source)
XLA Modules:
  0.0 98.2 jit_solution(1509559146807635975)
XLA Ops:
  0.6 94.7 %shard_map.95 = (bf16[256,1792]{1,0:T(8,128)(2,1)}, f32[32,1792]{1,0:T(8,128)}) custom-call(s32[8,256]{1,0:T(8,128)} %bitcast.2, s32[8,256]{1,0:T(8,128)} %bitcast.3, bf16[32,1792]{1,0:T(8,128)(2,1)} %proj_hbm.1, bf16[256,1792]{1,0:T(8,128)(2,1)} %teacher_hbm.1, bf16[256,2048]{1,0:T(8,128)(2,1)} %student_hbm.1, bf16[1792,512]{1,0:T(8,128)(2,1)} %wg_hbm.1, ...), custom_call_target="tpu_custom_call" | custom-call | flops 8000000000 | bytes 12000000 | tf_op jit(solution)/shard_map/pallas_call | solution.py:456
  95.3 0.0 copy-start
  95.3 2.2 %copy.12 = bf16[256,1792]{1,0:T(8,128)(2,1)} copy(bf16[256,1792]{1,0:T(8,128)(2,1)} %get-tuple-element.4) | data formatting | bytes 1835008
  97.5 0.0 copy-done
  97.5 0.7 copy.13
Async XLA Ops:
  95.3 2.2 %copy-start = (f32[32,1792]{1,0:T(8,128)S(1)}, f32[32,1792]{1,0:T(8,128)}, u32[]{:S(2)}) copy-start(f32[32,1792]{1,0:T(8,128)} %get-tuple-element.5) | copy-start | bytes 688132

commit v3 on v2

--- a/solution.py
+++ b/solution.py
@@ -26,11 +26,8 @@
 
 
 def tiles(count, size, f, first=0):
-    def step(i, carry):
-        f(pl.ds(pl.multiple_of(first + i * size, 128), size))
-        return carry
-
-    lax.fori_loop(0, count, step, 0)
+    for i in range(count):
+        f(pl.ds(first + i * size, size))
 
 
 def kernel(
@@ -116,12 +113,14 @@
     chosen = chosen.astype(BF)
 
     def pack(cols):
-        low = dot(chosen, teacher[:, cols]).reshape(16, 8, 128)
-        high = dot(chosen, teacher[:, pl.ds(pl.multiple_of(896 + cols.start, 128), 128)]).reshape(16, 8, 128)
+        size = cols.size
+        low = dot(chosen, teacher[:, cols]).reshape(16, 8, size)
+        high = dot(chosen, teacher[:, pl.ds(896 + cols.start, size)]).reshape(16, 8, size)
         packed[:, :, cols] = jnp.concatenate([low, high], axis=1).astype(BF)
 
     operands[2].wait()
-    tiles(7, 128, pack)
+    tiles(3, 256, pack)
+    tiles(1, 128, pack, 768)
     pl.semaphore_wait(barrier, len(peers))
 
     out_hop = (0, -1, 2, -3)
@@ -155,13 +154,14 @@
 
     gram = {}
 
-    def gram_start():
-        tiles(8, 256, early)
-        gram["core"] = copy_to(gx.at[:, 1 - c], gxr, at(other=True))
+    def gram_part(q):
+        tiles(2, 256, early, q * 512)
+        cols = pl.ds(q * 512, 512)
+        gram["core", q] = copy_to(gx.at[:, 1 - c, :, cols], gxr.at[:, :, cols], at(other=True))
 
     def gram_0():
-        gram["core"].wait_recv()
         for q in range(4):
+            gram["core", q].wait_recv()
             cols = slice(q * 512, q * 512 + 512)
             gs1[q] = (gx[:, c, :, cols].astype(F32) + gxr[:, :, cols].astype(F32)).astype(BF)
         gram["y"] = [copy_to(gs1.at[(y + d) % 4], gr1.at[d], at(dy=d)) for d in (1, 3, 2)]
@@ -226,7 +226,7 @@
         swap.append(copy_to(gtt.at[:, 1 - c], gtf.at[:, :, other_k], at(other=True)))
 
     to_x, act_x, back_core, back_pair, back_z, round_y, far_y, whole = {}, {}, {}, {}, {}, {}, {}, {}
-    parts = ((0, 4), (1024, 3))
+    parts = ((0, 3), (768, 2), (1280, 2))
 
     def spans(j):
         return parts if j == 3 else ((0, 7),)
@@ -250,18 +250,14 @@
         def unfold(cols):
             block = rows[:, j, :, :, :, cols].astype(F32).reshape(16, 2, 8, 128)
             xk[:, cols] = block[:, 0].reshape(128, 128).astype(BF)
-            xk[:, pl.ds(pl.multiple_of(896 + cols.start, 128), 128)] = block[:, 1].reshape(128, 128).astype(BF)
+            xk[:, pl.ds(896 + cols.start, 128)] = block[:, 1].reshape(128, 128).astype(BF)
 
         tiles(7, 128, unfold)
         if j == 0:
             weights[0].wait()
             weights[1].wait()
         for part in range(2):
-            def step(cols):
-                out = dot(xk[...], wgu[part, :, cols])
-                gu[j, part, :, :, cols] = out.reshape(4, 32, 256).astype(BF)
-
-            tiles(2, 256, step)
+            gu[j, part] = dot(xk[...], wgu[part]).reshape(4, 32, H).astype(BF)
         to_x[j] = [copy_to(gu.at[j, :, (x + d) % 4], xr.at[j, d], at_x(d)) for d in (1, 3, 2)]
 
     def activate(j):
@@ -367,13 +363,14 @@
         return (lambda _: f(), 0)
 
     run([
-        when(wn_rows), (arrive, 0), (arrive_via, 0), when(gram_start), (arrive, 1), (arrive, 2), when(send_proj),
-        (wn_send, 3), (gate_up, 0), (arrive_via, 1), (wn_send, 1), (arrive, 3), (wn_send, 2), (gate_up, 1),
-        (arrive_via, 2), (activate, 0), when(gram_0), (gate_up, 2), (arrive_via, 3), (activate, 1), (down, 0),
-        (gate_up, 3), (core_sum, 0), (activate, 2), (down, 1), (wn_send, 0), (core_sum, 1), (activate, 3),
-        (pair_sum, 0), (down, 2), (core_sum, 2), (pair_sum, 1), (down, 3), (relay, 0), (core_sum, 3), when(gram_1),
-        (pair_sum, 2), when(student_rows), (far, 0), when(swap_proj), (pair_sum, 3), (relay, 2), (relay, 1),
-        (relay, 3), when(gram_2), (far, 2), (far, 1), when(gram_3), (far, 3), when(student),
+        when(send_proj), (arrive, 0), (arrive_via, 0), (arrive, 1), when(wn_rows), (gram_part, 3), (gram_part, 2),
+        (arrive, 2), (wn_send, 0), (gate_up, 0), (arrive_via, 1), (gram_part, 1), (arrive_via, 2), (gram_part, 0),
+        (gate_up, 1), (gate_up, 2), (arrive, 3), (activate, 0), (wn_send, 1), when(gram_0), (wn_send, 2),
+        (activate, 2), (arrive_via, 3), (down, 0), (activate, 1), (down, 2), (wn_send, 3), (core_sum, 0), (down, 1),
+        (core_sum, 2), (gate_up, 3), when(swap_proj), (pair_sum, 0), (core_sum, 1), when(gram_1), (pair_sum, 2),
+        (activate, 3), (relay, 0), when(student_rows), (pair_sum, 1), (down, 3), (relay, 2), (far, 0), (relay, 1),
+        (core_sum, 3), (far, 2), when(gram_2), (far, 1), (pair_sum, 3), when(gram_3), (relay, 3), (far, 3),
+        when(student),
     ])
 
     to_owner = []
@@ -420,9 +417,9 @@
         if step == 0:
             send_target()
         if step == 1:
-            for copy in started[:-8]:
+            for copy in started[:-10]:
                 copy.wait_send()
-            del started[:-8]
+            del started[:-10]
         if step == 2:
             for copy in to_owner:
                 copy.wait_recv()
@@ -448,7 +445,7 @@
     grad_out.wait()
 
 
-N_COPIES = 19 + 3 + 8 + 12 + 12 + 5 + 5 + 3 + 40 + 3 + 15 + 14 + 3 + 3 + 16
+N_COPIES = 40 + 19 + 3 + 8 + 12 + 12 + 5 + 5 + 3 + 40 + 3 + 15 + 14 + 3 + 3 + 16
 
 
 def body(teacher_in, expert_ids, gate_codes, w_gate, w_up, w_down, student_in, projection):

time: 98.4 us -> 96.3 us (0.979)
  the two profiles are of different devices: /device:TPU:1 before, /device:TPU:8 now
where the time goes in v3:
time: 96.3 us; the launch traced here: 96.2 us
  Pallas kernels  92.6 us (96%)
  local copies, waits for them, and re-layouts  2.89 us (3%)
    pallas_call x1, Pallas kernels, body(): pl.pallas_call(kernel, out_shape=(jax.ShapeDtypeStruct((256, W), BF), jax...  92.6 us
    unnamed x4, local copies, waits for them, and re-layouts  2.89 us

profile of v3, /device:TPU:8, one launch (start us, length us, event | category | flops | bytes accessed | tf_op | source)
XLA Modules:
  0.0 96.2 jit_solution(9329254202964575597)
XLA Ops:
  0.6 92.6 %shard_map.95 = (bf16[256,1792]{1,0:T(8,128)(2,1)}, f32[32,1792]{1,0:T(8,128)}) custom-call(s32[8,256]{1,0:T(8,128)} %bitcast.2, s32[8,256]{1,0:T(8,128)} %bitcast.3, bf16[32,1792]{1,0:T(8,128)(2,1)} %proj_hbm.1, bf16[256,1792]{1,0:T(8,128)(2,1)} %teacher_hbm.1, bf16[256,2048]{1,0:T(8,128)(2,1)} %student_hbm.1, bf16[1792,512]{1,0:T(8,128)(2,1)} %wg_hbm.1, ...), custom_call_target="tpu_custom_call" | custom-call | flops 8000000000 | bytes 12000000 | tf_op jit(solution)/shard_map/pallas_call | solution.py:453
  93.3 0.0 copy-start
  93.3 2.2 %copy.12 = bf16[256,1792]{1,0:T(8,128)(2,1)} copy(bf16[256,1792]{1,0:T(8,128)(2,1)} %get-tuple-element.4) | data formatting | bytes 1835008
  95.5 0.0 copy-done
  95.5 0.7 copy.13
Async XLA Ops:
  93.3 2.2 %copy-start = (f32[32,1792]{1,0:T(8,128)S(1)}, f32[32,1792]{1,0:T(8,128)}, u32[]{:S(2)}) copy-start(f32[32,1792]{1,0:T(8,128)} %get-tuple-element.5) | copy-start | bytes 688132

commit v4 on v3

--- a/solution.py
+++ b/solution.py
@@ -34,7 +34,7 @@
     ids_hbm, codes_hbm, proj_hbm, teacher_hbm, student_hbm, wg_hbm, wu_hbm, wd_hbm,
     target_hbm, grad_hbm, target, grad, tg, ids, codes, proj, teacher, student_in,
     wgu, wd, weigh, packed, normed, left_x, wn, gx, rows, xk, gu, xr, act, prodf, ps, pr, vs, vr, ob, ret, tb,
-    wnb, pb, gxr, gs1, gr1, gs2, gr2, gt, gtt, gtf, wkt, wk, m, zs, zr,
+    wny, wnb, pb, gxr, gs1, gr1, gs2, gr2, gs3, gr3, gt, gtt, gtf, wkt, wk, m, zs, zr,
     send_sem, recv_sem, local_sem,
 ):
     e = lax.axis_index("exp")
@@ -42,12 +42,21 @@
     y, z, c = e // 16, (e // 2) % 8, e % 2
     sg = 1 - 2 * (z % 2)
 
-    def at(dy=0, dz=0, other=False):
-        yy, zz = (y + dy + 4) % 4, (z + dz + 8) % 8
-        return (yy * 16 + zz * 2 + (1 - c if other else c), x)
+    by_y = [lax.rem(y + d, 4) for d in range(4)]
+    by_x = [lax.rem(x + d, 4) for d in range(4)]
+    by_z = [lax.rem(z + d, 8) for d in range(8)]
+    by_hop = {d: lax.rem(z + d * sg + 8, 8) for d in (1, -1, 2, -2, 3, -3)}
+    known = {}
+
+    def at(dy=0, dz=0, hop=0, other=False):
+        key = dy % 4, dz % 8, hop, other
+        if key not in known:
+            zz = by_hop[hop] if hop else by_z[dz % 8]
+            known[key] = (by_y[dy % 4] * 16 + zz * 2 + (1 - c if other else c), x)
+        return known[key]
 
     def at_x(dx):
-        return (e, (x + dx) % 4)
+        return (e, by_x[dx % 4])
 
     number = [0, 0]
     started = []
@@ -124,16 +133,16 @@
     pl.semaphore_wait(barrier, len(peers))
 
     out_hop = (0, -1, 2, -3)
-    direct, via, over, over_via = {}, {}, {}, {}
+    direct, via, over = {}, {}, {}
     for j in range(4):
         direct[j] = new_recv()
         for d in (1, 3, 2, 0):
             if j or d:
-                copy_to(packed.at[d * 4 + j], rows.at[0, j, 0, d], at(dy=-d, dz=out_hop[j] * sg), direct[j])
+                copy_to(packed.at[d * 4 + j], rows.at[0, j, 0, d], at(dy=-d, hop=out_hop[j]), direct[j])
         if j == 0:
             via[0] = new_recv()
             for d in (0, 1, 3, 2):
-                copy_to(packed.at[d * 4], rows.at[1, 0, 0, d], at(dy=-d, dz=sg), via[0])
+                copy_to(packed.at[d * 4], rows.at[1, 0, 0, d], at(dy=-d, hop=1), via[0])
     rows[0, 0, 0, 0] = packed[0]
     for copy in weights:
         copy.start()
@@ -154,29 +163,33 @@
 
     gram = {}
 
-    def gram_part(q):
-        tiles(2, 256, early, q * 512)
-        cols = pl.ds(q * 512, 512)
-        gram["core", q] = copy_to(gx.at[:, 1 - c, :, cols], gxr.at[:, :, cols], at(other=True))
+    def gram_start():
+        tiles(8, 256, early)
+        gram["core"] = copy_to(gx.at[:, 1 - c], gxr, at(other=True))
 
     def gram_0():
+        gram["core"].wait_recv()
         for q in range(4):
-            gram["core", q].wait_recv()
             cols = slice(q * 512, q * 512 + 512)
             gs1[q] = (gx[:, c, :, cols].astype(F32) + gxr[:, :, cols].astype(F32)).astype(BF)
-        gram["y"] = [copy_to(gs1.at[(y + d) % 4], gr1.at[d], at(dy=d)) for d in (1, 3, 2)]
+        gram["y"] = [copy_to(gs1.at[by_y[d]], gr1.at[d], at(dy=d)) for d in (1, 3, 2)]
 
     def gram_1():
         for copy in gram["y"]:
             copy.wait_recv()
         total = gs1[y].astype(F32) + sum(gr1[d].astype(F32) for d in (1, 2, 3))
-        gs2[...] = total.astype(BF)
-        gram["z"] = [copy_to(gs2.at[(z + d) % 8], gr2.at[d], at(dz=d)) for d in (1, 7, 2, 6, 3, 5, 4)]
+        gs2[...] = total.astype(BF).reshape(4, 2, 32, 512)
+        gram["pair"] = copy_to(gs2.at[:, 1 - z % 2], gr2, at(hop=1))
+
+    def gram_1b():
+        gram["pair"].wait_recv()
+        gs3[...] = (gs2[:, z % 2].astype(F32) + gr2[...].astype(F32)).astype(BF)
+        gram["z"] = [copy_to(gs3.at[by_z[d] // 2], gr3.at[d // 2], at(dz=d)) for d in (2, 6, 4)]
 
     def gram_2():
         for copy in gram["z"]:
             copy.wait_recv()
-        total = gs2[z].astype(F32) + sum(gr2[d].astype(F32) for d in range(1, 8))
+        total = gs3[z // 2].astype(F32) + sum(gr3[d].astype(F32) for d in range(1, 4))
         gt[x] = total.astype(BF)
         gram["x"] = [copy_to(gt.at[x], gt.at[x], at_x(d)) for d in (1, 3, 2)]
 
@@ -187,19 +200,22 @@
         early_y.extend([copy_to(proj, pb.at[0, y], at(dy=d)) for d in (1, 3, 2)])
         pb[0, y] = proj[...]
 
+    wn_y, wn_z = [], {}
+
     def wn_rows():
         tiles(8, 256, early_rows)
 
-    early_wn = {}
+        def features(yy):
+            return pl.ds(pl.multiple_of(yy * 512, 512), 512)
+
+        wn_y.extend([copy_to(wn.at[:, :, features(by_y[4 - d])], wny.at[d], at(dy=-d)) for d in (1, 3, 2)])
+        wny[0] = wn[:, :, features(y)]
 
     def wn_send(j):
-        early_wn[j] = new_recv()
-        for d in (0, 1, 3, 2):
-            cols = pl.ds(pl.multiple_of(((y + 4 - d) % 4) * 512, 512), 512)
-            if j == 0 and d == 0:
-                wnb[0, 0] = wn[0, :, cols]
-            else:
-                copy_to(wn.at[j, :, cols], wnb.at[j, d], at(dy=-d, dz=out_hop[j] * sg), early_wn[j])
+        while wn_y:
+            wn_y.pop().wait_recv()
+        if j:
+            wn_z[j] = copy_to(wny.at[:, j], wnb.at[j], at(hop=out_hop[j]))
 
     def swap_proj():
         for copy in early_y:
@@ -210,9 +226,9 @@
 
     def student_rows():
         for j in range(4):
-            into = wnb.at[j, pl.ds(1, 3)] if j == 0 else wnb.at[j]
-            arrival(into, early_wn[j]).wait_recv()
-            blocks = [wnb[j, d].astype(F32) for d in range(4)]
+            if j:
+                wn_z[j].wait_recv()
+            blocks = [(wnb[j, d] if j else wny[d, 0]).astype(F32) for d in range(4)]
             order = [blocks[(d + 4 - g) % 4][d * 8:d * 8 + 8] for g in range(4) for d in range(4)]
             wkt[j] = jnp.concatenate(order, axis=0).T.reshape(8, 2, 32, 128).astype(BF)
             wk[j, :, :, 0:128] = wkt[j, :, c]
@@ -226,7 +242,7 @@
         swap.append(copy_to(gtt.at[:, 1 - c], gtf.at[:, :, other_k], at(other=True)))
 
     to_x, act_x, back_core, back_pair, back_z, round_y, far_y, whole = {}, {}, {}, {}, {}, {}, {}, {}
-    parts = ((0, 3), (768, 2), (1280, 2))
+    parts = ((0, 4), (1024, 3))
 
     def spans(j):
         return parts if j == 3 else ((0, 7),)
@@ -236,16 +252,14 @@
         arrival(into, direct[j]).wait_recv()
         if j:
             via[j] = new_recv()
-            copy_to(rows.at[0, j, 0], rows.at[1, j, 0], at(dz=sg), via[j])
-        over[j] = copy_to(rows.at[0, j, 0], rows.at[0, j, 1], at(other=True))
+            copy_to(rows.at[0, j, 0], rows.at[1, j, 0], at(hop=1), via[j])
 
     def arrive_via(j):
         arrival(rows.at[1, j, 0], via[j]).wait_recv()
-        over_via[j] = copy_to(rows.at[1, j, 0], rows.at[1, j, 1], at(other=True))
+        over[j] = copy_to(rows.at[:, j, 0], rows.at[:, j, 1], at(other=True))
 
     def gate_up(j):
         over[j].wait_recv()
-        over_via[j].wait_recv()
 
         def unfold(cols):
             block = rows[:, j, :, :, :, cols].astype(F32).reshape(16, 2, 8, 128)
@@ -258,7 +272,7 @@
             weights[1].wait()
         for part in range(2):
             gu[j, part] = dot(xk[...], wgu[part]).reshape(4, 32, H).astype(BF)
-        to_x[j] = [copy_to(gu.at[j, :, (x + d) % 4], xr.at[j, d], at_x(d)) for d in (1, 3, 2)]
+        to_x[j] = [copy_to(gu.at[j, :, by_x[d]], xr.at[j, d], at_x(d)) for d in (1, 3, 2)]
 
     def activate(j):
         for copy in to_x[j]:
@@ -294,7 +308,7 @@
             back_core[j, first].wait_recv()
             tiles(count, 256, step, first)
             cols = pl.ds(first, count * 256)
-            back_pair[j, first] = copy_to(vs.at[j, :, cols], vr.at[j, :, cols], at(dz=sg))
+            back_pair[j, first] = copy_to(vs.at[j, :, cols], vr.at[j, :, cols], at(hop=1))
 
     def pair_sum(j):
         def step(cols):
@@ -310,7 +324,7 @@
                 copy_to(ob.at[j, 0, 0, :, cols], ob.at[j, 0, g, :, cols], at(dy=g)) for g in (1, 3)
             ]
         if j:
-            back_z[j] = copy_to(ob.at[j, 0, 0], ret.at[j], at(dz=-j * sg))
+            back_z[j] = copy_to(ob.at[j, 0, 0], ret.at[j], at(hop=-j))
 
     def relay(j):
         low, high = pl.ds(0, 16), pl.ds(16, 16)
@@ -363,14 +377,13 @@
         return (lambda _: f(), 0)
 
     run([
-        when(send_proj), (arrive, 0), (arrive_via, 0), (arrive, 1), when(wn_rows), (gram_part, 3), (gram_part, 2),
-        (arrive, 2), (wn_send, 0), (gate_up, 0), (arrive_via, 1), (gram_part, 1), (arrive_via, 2), (gram_part, 0),
-        (gate_up, 1), (gate_up, 2), (arrive, 3), (activate, 0), (wn_send, 1), when(gram_0), (wn_send, 2),
-        (activate, 2), (arrive_via, 3), (down, 0), (activate, 1), (down, 2), (wn_send, 3), (core_sum, 0), (down, 1),
-        (core_sum, 2), (gate_up, 3), when(swap_proj), (pair_sum, 0), (core_sum, 1), when(gram_1), (pair_sum, 2),
-        (activate, 3), (relay, 0), when(student_rows), (pair_sum, 1), (down, 3), (relay, 2), (far, 0), (relay, 1),
-        (core_sum, 3), (far, 2), when(gram_2), (far, 1), (pair_sum, 3), when(gram_3), (relay, 3), (far, 3),
-        when(student),
+        (arrive, 0), (arrive_via, 0), (arrive, 1), when(gram_start), (arrive, 2), (gate_up, 0), (arrive_via, 1),
+        when(wn_rows), (arrive, 3), (arrive_via, 2), when(gram_0), (activate, 0), (gate_up, 1), (gate_up, 2),
+        (wn_send, 2), (down, 0), when(send_proj), (arrive_via, 3), (activate, 1), (core_sum, 0), (wn_send, 3),
+        (gate_up, 3), (down, 1), (activate, 2), (core_sum, 1), when(gram_1), (pair_sum, 0), (wn_send, 0),
+        (activate, 3), (down, 2), (wn_send, 1), when(swap_proj), (pair_sum, 1), (core_sum, 2), (down, 3), (relay, 0),
+        (core_sum, 3), (relay, 1), when(gram_1b), (pair_sum, 2), (far, 0), (pair_sum, 3), when(student_rows),
+        (far, 1), (relay, 2), when(gram_2), (relay, 3), (far, 2), when(gram_3), (far, 3), when(student),
     ])
 
     to_owner = []
@@ -389,7 +402,7 @@
         tg[0] = tb[0]
 
     def mine(d, first, count, cols):
-        return m[(z + 8 + d) % 8, first:first + count, cols]
+        return m[by_z[d % 8], first:first + count, cols]
 
     hops = {}
     for step in range(4):
@@ -417,9 +430,9 @@
         if step == 0:
             send_target()
         if step == 1:
-            for copy in started[:-10]:
+            for copy in started[:-8]:
                 copy.wait_send()
-            del started[:-10]
+            del started[:-8]
         if step == 2:
             for copy in to_owner:
                 copy.wait_recv()
@@ -445,7 +458,7 @@
     grad_out.wait()
 
 
-N_COPIES = 40 + 19 + 3 + 8 + 12 + 12 + 5 + 5 + 3 + 40 + 3 + 15 + 14 + 3 + 3 + 16
+N_COPIES = 140
 
 
 def body(teacher_in, expert_ids, gate_codes, w_gate, w_up, w_down, student_in, projection):
@@ -489,12 +502,15 @@
             pltpu.VMEM((4, 32, W), BF),
             pltpu.VMEM((4, 32, W), BF),
             pltpu.VMEM((4, 4, 32, 512), BF),
+            pltpu.VMEM((4, 4, 32, 512), BF),
             pltpu.VMEM((2, 4, 32, W), BF),
             pltpu.VMEM((8, 32, 2048), BF),
             pltpu.VMEM((4, 8, 32, 512), BF),
             pltpu.VMEM((4, 8, 32, 512), BF),
-            pltpu.VMEM((8, 32, 512), BF),
-            pltpu.VMEM((8, 32, 512), BF),
+            pltpu.VMEM((4, 2, 32, 512), BF),
+            pltpu.VMEM((4, 32, 512), BF),
+            pltpu.VMEM((4, 32, 512), BF),
+            pltpu.VMEM((4, 32, 512), BF),
             pltpu.VMEM((4, 32, 512), BF),
             pltpu.VMEM((8, 2, 32, 128), BF),
             pltpu.VMEM((8, 32, 256), BF),

time: 96.3 us -> 92 us (0.955)
  the two profiles are of different devices: /device:TPU:8 before, /device:TPU:1 now
where the time goes in v4:
time: 92 us; the launch traced here: 91.9 us
  Pallas kernels  88.4 us (96%)
  local copies, waits for them, and re-layouts  2.89 us (3%)
    pallas_call x1, Pallas kernels, body(): pl.pallas_call(kernel, out_shape=(jax.ShapeDtypeStruct((256, W), BF), jax...  88.4 us
    unnamed x4, local copies, waits for them, and re-layouts  2.89 us

profile of v4, /device:TPU:1, one launch (start us, length us, event | category | flops | bytes accessed | tf_op | source)
XLA Modules:
  0.0 91.9 jit_solution(16517898693522928031)
XLA Ops:
  0.6 88.4 %shard_map.95 = (bf16[256,1792]{1,0:T(8,128)(2,1)}, f32[32,1792]{1,0:T(8,128)}) custom-call(s32[8,256]{1,0:T(8,128)} %bitcast.2, s32[8,256]{1,0:T(8,128)} %bitcast.3, bf16[32,1792]{1,0:T(8,128)(2,1)} %proj_hbm.1, bf16[256,1792]{1,0:T(8,128)(2,1)} %teacher_hbm.1, bf16[256,2048]{1,0:T(8,128)(2,1)} %student_hbm.1, bf16[1792,512]{1,0:T(8,128)(2,1)} %wg_hbm.1, ...), custom_call_target="tpu_custom_call" | custom-call | flops 8000000000 | bytes 12000000 | tf_op jit(solution)/shard_map/pallas_call | solution.py:466
  89.0 0.0 copy-start
  89.0 2.2 %copy.12 = bf16[256,1792]{1,0:T(8,128)(2,1)} copy(bf16[256,1792]{1,0:T(8,128)(2,1)} %get-tuple-element.4) | data formatting | bytes 1835008
  91.2 0.0 copy-done
  91.2 0.7 copy.13
Async XLA Ops:
  89.0 2.2 %copy-start = (f32[32,1792]{1,0:T(8,128)S(1)}, f32[32,1792]{1,0:T(8,128)}, u32[]{:S(2)}) copy-start(f32[32,1792]{1,0:T(8,128)} %get-tuple-element.5) | copy-start | bytes 688132

commit v5 on v4

--- a/solution.py
+++ b/solution.py
@@ -26,8 +26,11 @@
 
 
 def tiles(count, size, f, first=0):
-    for i in range(count):
-        f(pl.ds(first + i * size, size))
+    def step(i, carry):
+        f(pl.ds(pl.multiple_of(first + i * size, 128), size))
+        return carry
+
+    lax.fori_loop(0, count, step, 0)
 
 
 def kernel(
@@ -65,23 +68,31 @@
         number[1] += 1
         return number[1] - 1
 
-    def copy_to(src, dst, device, recv=None):
-        i = number[0]
+    def new_send():
         number[0] += 1
-        copy = pltpu.make_async_remote_copy(
-            src_ref=src, dst_ref=dst, send_sem=send_sem.at[i],
-            recv_sem=recv_sem.at[new_recv() if recv is None else recv],
+        return number[0] - 1
+
+    def describe(src, dst, device, send, recv):
+        return pltpu.make_async_remote_copy(
+            src_ref=src, dst_ref=dst, send_sem=send_sem.at[send], recv_sem=recv_sem.at[recv],
             device_id=device, device_id_type=MESH,
         )
+
+    def copy_to(src, dst, device, recv=None):
+        copy = describe(src, dst, device, new_send(), new_recv() if recv is None else recv)
         copy.start()
         started.append(copy)
         return copy
 
+    def group(copies, whole):
+        send, recv = new_send(), new_recv()
+        for src, dst, device in copies:
+            describe(src, dst, device, send, recv).start()
+        started.append(describe(whole, whole, at(other=True), send, recv))
+        return started[-1]
+
     def arrival(dst, recv):
-        return pltpu.make_async_remote_copy(
-            src_ref=dst, dst_ref=dst, send_sem=send_sem.at[0], recv_sem=recv_sem.at[recv],
-            device_id=at(other=True), device_id_type=MESH,
-        )
+        return describe(dst, dst, at(other=True), 0, recv)
 
     weights = [
         pltpu.make_async_copy(wg_hbm, wgu.at[0], local_sem.at[0]),
@@ -124,7 +135,7 @@
     def pack(cols):
         size = cols.size
         low = dot(chosen, teacher[:, cols]).reshape(16, 8, size)
-        high = dot(chosen, teacher[:, pl.ds(896 + cols.start, size)]).reshape(16, 8, size)
+        high = dot(chosen, teacher[:, pl.ds(pl.multiple_of(896 + cols.start, 128), size)]).reshape(16, 8, size)
         packed[:, :, cols] = jnp.concatenate([low, high], axis=1).astype(BF)
 
     operands[2].wait()
@@ -134,15 +145,20 @@
 
     out_hop = (0, -1, 2, -3)
     direct, via, over = {}, {}, {}
-    for j in range(4):
+    first, second = new_send(), new_send()
+    for j in (0, 1, 2, 3):
         direct[j] = new_recv()
         for d in (1, 3, 2, 0):
             if j or d:
-                copy_to(packed.at[d * 4 + j], rows.at[0, j, 0, d], at(dy=-d, hop=out_hop[j]), direct[j])
+                describe(
+                    packed.at[d * 4 + j], rows.at[0, j, 0, d], at(dy=-d, hop=out_hop[j]), first, direct[j]
+                ).start()
         if j == 0:
             via[0] = new_recv()
             for d in (0, 1, 3, 2):
-                copy_to(packed.at[d * 4], rows.at[1, 0, 0, d], at(dy=-d, hop=1), via[0])
+                describe(packed.at[d * 4], rows.at[1, 0, 0, d], at(dy=-d, hop=1), second, via[0]).start()
+    started.append(describe(packed.at[pl.ds(0, 15)], packed.at[pl.ds(0, 15)], at(other=True), first, direct[0]))
+    started.append(describe(packed.at[pl.ds(0, 4)], packed.at[pl.ds(0, 4)], at(other=True), second, via[0]))
     rows[0, 0, 0, 0] = packed[0]
     for copy in weights:
         copy.start()
@@ -172,11 +188,10 @@
         for q in range(4):
             cols = slice(q * 512, q * 512 + 512)
             gs1[q] = (gx[:, c, :, cols].astype(F32) + gxr[:, :, cols].astype(F32)).astype(BF)
-        gram["y"] = [copy_to(gs1.at[by_y[d]], gr1.at[d], at(dy=d)) for d in (1, 3, 2)]
+        gram["y"] = group([(gs1.at[by_y[d]], gr1.at[d], at(dy=d)) for d in (1, 3, 2)], gr1.at[pl.ds(1, 3)])
 
     def gram_1():
-        for copy in gram["y"]:
-            copy.wait_recv()
+        gram["y"].wait_recv()
         total = gs1[y].astype(F32) + sum(gr1[d].astype(F32) for d in (1, 2, 3))
         gs2[...] = total.astype(BF).reshape(4, 2, 32, 512)
         gram["pair"] = copy_to(gs2.at[:, 1 - z % 2], gr2, at(hop=1))
@@ -184,20 +199,21 @@
     def gram_1b():
         gram["pair"].wait_recv()
         gs3[...] = (gs2[:, z % 2].astype(F32) + gr2[...].astype(F32)).astype(BF)
-        gram["z"] = [copy_to(gs3.at[by_z[d] // 2], gr3.at[d // 2], at(dz=d)) for d in (2, 6, 4)]
+        gram["z"] = group(
+            [(gs3.at[by_z[d] // 2], gr3.at[d // 2], at(dz=d)) for d in (2, 6, 4)], gr3.at[pl.ds(1, 3)]
+        )
 
     def gram_2():
-        for copy in gram["z"]:
-            copy.wait_recv()
+        gram["z"].wait_recv()
         total = gs3[z // 2].astype(F32) + sum(gr3[d].astype(F32) for d in range(1, 4))
         gt[x] = total.astype(BF)
-        gram["x"] = [copy_to(gt.at[x], gt.at[x], at_x(d)) for d in (1, 3, 2)]
+        gram["x"] = group([(gt.at[x], gt.at[x], at_x(d)) for d in (1, 3, 2)], gt.at[pl.ds(0, 3)])
 
     early_y, swap = [], []
 
     def send_proj():
         operands[4].wait()
-        early_y.extend([copy_to(proj, pb.at[0, y], at(dy=d)) for d in (1, 3, 2)])
+        early_y.append(group([(proj, pb.at[0, y], at(dy=d)) for d in (1, 3, 2)], pb.at[0, pl.ds(0, 3)]))
         pb[0, y] = proj[...]
 
     wn_y, wn_z = [], {}
@@ -208,7 +224,9 @@
         def features(yy):
             return pl.ds(pl.multiple_of(yy * 512, 512), 512)
 
-        wn_y.extend([copy_to(wn.at[:, :, features(by_y[4 - d])], wny.at[d], at(dy=-d)) for d in (1, 3, 2)])
+        wn_y.append(group(
+            [(wn.at[:, :, features(by_y[4 - d])], wny.at[d], at(dy=-d)) for d in (1, 3, 2)], wny.at[pl.ds(1, 3)]
+        ))
         wny[0] = wn[:, :, features(y)]
 
     def wn_send(j):
@@ -235,8 +253,7 @@
         swap.append(copy_to(wkt.at[:, :, 1 - c], wk.at[:, :, :, other_k], at(other=True)))
 
     def gram_3():
-        for copy in gram["x"]:
-            copy.wait_recv()
+        gram["x"].wait_recv()
         gtt[...] = gt[...].reshape(128, 512).astype(F32).T.reshape(8, 2, 32, 128).astype(BF)
         gtf[:, :, 0:128] = gtt[:, c]
         swap.append(copy_to(gtt.at[:, 1 - c], gtf.at[:, :, other_k], at(other=True)))
@@ -264,7 +281,7 @@
         def unfold(cols):
             block = rows[:, j, :, :, :, cols].astype(F32).reshape(16, 2, 8, 128)
             xk[:, cols] = block[:, 0].reshape(128, 128).astype(BF)
-            xk[:, pl.ds(896 + cols.start, 128)] = block[:, 1].reshape(128, 128).astype(BF)
+            xk[:, pl.ds(pl.multiple_of(896 + cols.start, 128), 128)] = block[:, 1].reshape(128, 128).astype(BF)
 
         tiles(7, 128, unfold)
         if j == 0:
@@ -272,20 +289,18 @@
             weights[1].wait()
         for part in range(2):
             gu[j, part] = dot(xk[...], wgu[part]).reshape(4, 32, H).astype(BF)
-        to_x[j] = [copy_to(gu.at[j, :, by_x[d]], xr.at[j, d], at_x(d)) for d in (1, 3, 2)]
+        to_x[j] = group([(gu.at[j, :, by_x[d]], xr.at[j, d], at_x(d)) for d in (1, 3, 2)], xr.at[j, pl.ds(1, 3)])
 
     def activate(j):
-        for copy in to_x[j]:
-            copy.wait_recv()
+        to_x[j].wait_recv()
         gate, up = [
             gu[j, part, x].astype(F32) + sum(xr[j, d, part].astype(F32) for d in (1, 2, 3)) for part in range(2)
         ]
         act[j, x] = (gate / (1.0 + jnp.exp(-gate)) * up).astype(BF)
-        act_x[j] = [copy_to(act.at[j, x], act.at[j, x], at_x(d)) for d in (1, 3, 2)]
+        act_x[j] = group([(act.at[j, x], act.at[j, x], at_x(d)) for d in (1, 3, 2)], act.at[j, pl.ds(0, 3)])
 
     def down(j):
-        for copy in act_x[j]:
-            copy.wait_recv()
+        act_x[j].wait_recv()
         if j == 0:
             weights[2].wait()
 
@@ -398,7 +413,7 @@
                 tb[d, :, cols] = jnp.concatenate([b[d * 8:d * 8 + 8] for b in blocks], axis=0).astype(BF)
 
         tiles(7, 256, sort_rows)
-        to_owner.extend([copy_to(tb.at[d], tg.at[d], at(dy=d)) for d in (1, 3, 2)])
+        to_owner.append(group([(tb.at[d], tg.at[d], at(dy=d)) for d in (1, 3, 2)], tg.at[pl.ds(1, 3)]))
         tg[0] = tb[0]
 
     def mine(d, first, count, cols):
@@ -430,9 +445,9 @@
         if step == 0:
             send_target()
         if step == 1:
-            for copy in started[:-8]:
+            for copy in started[:-6]:
                 copy.wait_send()
-            del started[:-8]
+            del started[:-6]
         if step == 2:
             for copy in to_owner:
                 copy.wait_recv()

time: 92 us -> 95.7 us (1.040)
  Pallas kernels: 88.4 us -> 92 us
    pallas_call x1, Pallas kernels: 88.4 us -> 92 us  [body(): pl.pallas_call(kernel, out_shape=(jax.ShapeDtypeStruct((256, W), BF), jax...]
where the time goes in v5:
time: 95.7 us; the launch traced here: 95.6 us
  Pallas kernels  92 us (96%)
  local copies, waits for them, and re-layouts  2.89 us (3%)
    pallas_call x1, Pallas kernels, body(): pl.pallas_call(kernel, out_shape=(jax.ShapeDtypeStruct((256, W), BF), jax...  92 us
    unnamed x4, local copies, waits for them, and re-layouts  2.89 us

profile of v5, /device:TPU:1, one launch (start us, length us, event | category | flops | bytes accessed | tf_op | source)
XLA Modules:
  0.0 95.6 jit_solution(11104856681492594135)
XLA Ops:
  0.6 92.0 %shard_map.95 = (bf16[256,1792]{1,0:T(8,128)(2,1)}, f32[32,1792]{1,0:T(8,128)}) custom-call(s32[8,256]{1,0:T(8,128)} %bitcast.2, s32[8,256]{1,0:T(8,128)} %bitcast.3, bf16[32,1792]{1,0:T(8,128)(2,1)} %proj_hbm.1, bf16[256,1792]{1,0:T(8,128)(2,1)} %teacher_hbm.1, bf16[256,2048]{1,0:T(8,128)(2,1)} %student_hbm.1, bf16[1792,512]{1,0:T(8,128)(2,1)} %wg_hbm.1, ...), custom_call_target="tpu_custom_call" | custom-call | flops 8000000000 | bytes 12000000 | tf_op jit(solution)/shard_map/pallas_call | solution.py:481
  92.7 0.0 copy-start
  92.7 2.2 %copy.12 = bf16[256,1792]{1,0:T(8,128)(2,1)} copy(bf16[256,1792]{1,0:T(8,128)(2,1)} %get-tuple-element.4) | data formatting | bytes 1835008
  94.9 0.0 copy-done
  94.9 0.7 copy.13
Async XLA Ops:
  92.7 2.2 %copy-start = (f32[32,1792]{1,0:T(8,128)S(1)}, f32[32,1792]{1,0:T(8,128)}, u32[]{:S(2)}) copy-start(f32[32,1792]{1,0:T(8,128)} %get-tuple-element.5) | copy-start | bytes 688132

commit v6 on v5

--- a/solution.py
+++ b/solution.py
@@ -26,11 +26,8 @@
 
 
 def tiles(count, size, f, first=0):
-    def step(i, carry):
-        f(pl.ds(pl.multiple_of(first + i * size, 128), size))
-        return carry
-
-    lax.fori_loop(0, count, step, 0)
+    for i in range(count):
+        f(pl.ds(first + i * size, size))
 
 
 def kernel(
@@ -95,8 +92,8 @@
         return describe(dst, dst, at(other=True), 0, recv)
 
     weights = [
-        pltpu.make_async_copy(wg_hbm, wgu.at[0], local_sem.at[0]),
-        pltpu.make_async_copy(wu_hbm, wgu.at[1], local_sem.at[1]),
+        pltpu.make_async_copy(wg_hbm, wgu.at[:, pl.ds(0, H)], local_sem.at[0]),
+        pltpu.make_async_copy(wu_hbm, wgu.at[:, pl.ds(H, H)], local_sem.at[1]),
         pltpu.make_async_copy(wd_hbm, wd, local_sem.at[2]),
     ]
     operands = [
@@ -135,7 +132,7 @@
     def pack(cols):
         size = cols.size
         low = dot(chosen, teacher[:, cols]).reshape(16, 8, size)
-        high = dot(chosen, teacher[:, pl.ds(pl.multiple_of(896 + cols.start, 128), size)]).reshape(16, 8, size)
+        high = dot(chosen, teacher[:, pl.ds(896 + cols.start, size)]).reshape(16, 8, size)
         packed[:, :, cols] = jnp.concatenate([low, high], axis=1).astype(BF)
 
     operands[2].wait()
@@ -281,21 +278,19 @@
         def unfold(cols):
             block = rows[:, j, :, :, :, cols].astype(F32).reshape(16, 2, 8, 128)
             xk[:, cols] = block[:, 0].reshape(128, 128).astype(BF)
-            xk[:, pl.ds(pl.multiple_of(896 + cols.start, 128), 128)] = block[:, 1].reshape(128, 128).astype(BF)
+            xk[:, pl.ds(896 + cols.start, 128)] = block[:, 1].reshape(128, 128).astype(BF)
 
         tiles(7, 128, unfold)
         if j == 0:
             weights[0].wait()
             weights[1].wait()
-        for part in range(2):
-            gu[j, part] = dot(xk[...], wgu[part]).reshape(4, 32, H).astype(BF)
-        to_x[j] = group([(gu.at[j, :, by_x[d]], xr.at[j, d], at_x(d)) for d in (1, 3, 2)], xr.at[j, pl.ds(1, 3)])
+        gu[j] = dot(xk[...], wgu[...]).reshape(4, 32, 2 * H).astype(BF)
+        to_x[j] = group([(gu.at[j, by_x[d]], xr.at[j, d], at_x(d)) for d in (1, 3, 2)], xr.at[j, pl.ds(1, 3)])
 
     def activate(j):
         to_x[j].wait_recv()
-        gate, up = [
-            gu[j, part, x].astype(F32) + sum(xr[j, d, part].astype(F32) for d in (1, 2, 3)) for part in range(2)
-        ]
+        total = gu[j, x].astype(F32) + sum(xr[j, d].astype(F32) for d in (1, 2, 3))
+        gate, up = total[:, :H], total[:, H:]
         act[j, x] = (gate / (1.0 + jnp.exp(-gate)) * up).astype(BF)
         act_x[j] = group([(act.at[j, x], act.at[j, x], at_x(d)) for d in (1, 3, 2)], act.at[j, pl.ds(0, 3)])
 
@@ -495,7 +490,7 @@
             pltpu.VMEM((32, W), BF),
             pltpu.VMEM((256, W), BF),
             pltpu.VMEM((256, 2048), BF),
-            pltpu.VMEM((2, W, H), BF),
+            pltpu.VMEM((W, 2 * H), BF),
             pltpu.VMEM((H, W), BF),
             pltpu.VMEM((128, 256), BF),
             pltpu.VMEM((16, 16, W // 2), BF),
@@ -505,8 +500,8 @@
             pltpu.VMEM((8, 2, 32, 2048), BF),
             pltpu.VMEM((2, 4, 2, 4, 16, W // 2), BF),
             pltpu.VMEM((128, W), BF),
-            pltpu.VMEM((4, 2, 4, 32, H), BF),
-            pltpu.VMEM((4, 4, 2, 32, H), BF),
+            pltpu.VMEM((4, 4, 32, 2 * H), BF),
+            pltpu.VMEM((4, 4, 32, 2 * H), BF),
             pltpu.VMEM((4, 4, 32, H), BF),
             pltpu.VMEM((4, 2, 32, W), F32),
             pltpu.VMEM((4, 2, 32, W), BF),

time: 95.7 us -> 92.1 us (0.962)
  Pallas kernels: 92 us -> 88.4 us
    pallas_call x1, Pallas kernels: 92 us -> 88.4 us  [body(): pl.pallas_call(kernel, out_shape=(jax.ShapeDtypeStruct((256, W), BF), jax...]
where the time goes in v6:
time: 92.1 us; the launch traced here: 92 us
  Pallas kernels  88.4 us (96%)
  local copies, waits for them, and re-layouts  2.89 us (3%)
    pallas_call x1, Pallas kernels, body(): pl.pallas_call(kernel, out_shape=(jax.ShapeDtypeStruct((256, W), BF), jax...  88.4 us
    unnamed x4, local copies, waits for them, and re-layouts  2.89 us

profile of v6, /device:TPU:1, one launch (start us, length us, event | category | flops | bytes accessed | tf_op | source)
XLA Modules:
  0.0 92.0 jit_solution(10313806402806385469)
XLA Ops:
  0.6 88.4 %shard_map.95 = (bf16[256,1792]{1,0:T(8,128)(2,1)}, f32[32,1792]{1,0:T(8,128)}) custom-call(s32[8,256]{1,0:T(8,128)} %bitcast.2, s32[8,256]{1,0:T(8,128)} %bitcast.3, bf16[32,1792]{1,0:T(8,128)(2,1)} %proj_hbm.1, bf16[256,1792]{1,0:T(8,128)(2,1)} %teacher_hbm.1, bf16[256,2048]{1,0:T(8,128)(2,1)} %student_hbm.1, bf16[1792,512]{1,0:T(8,128)(2,1)} %wg_hbm.1, ...), custom_call_target="tpu_custom_call" | custom-call | flops 8000000000 | bytes 12000000 | tf_op jit(solution)/shard_map/pallas_call | solution.py:476
  89.1 0.0 copy-start
  89.1 2.2 %copy.12 = bf16[256,1792]{1,0:T(8,128)(2,1)} copy(bf16[256,1792]{1,0:T(8,128)(2,1)} %get-tuple-element.4) | data formatting | bytes 1835008
  91.3 0.0 copy-done
  91.3 0.7 copy.13
Async XLA Ops:
  89.1 2.2 %copy-start = (f32[32,1792]{1,0:T(8,128)S(1)}, f32[32,1792]{1,0:T(8,128)}, u32[]{:S(2)}) copy-start(f32[32,1792]{1,0:T(8,128)} %get-tuple-element.5) | copy-start | bytes 688132

commit v7 on v4

--- a/solution.py
+++ b/solution.py
@@ -34,7 +34,7 @@
     ids_hbm, codes_hbm, proj_hbm, teacher_hbm, student_hbm, wg_hbm, wu_hbm, wd_hbm,
     target_hbm, grad_hbm, target, grad, tg, ids, codes, proj, teacher, student_in,
     wgu, wd, weigh, packed, normed, left_x, wn, gx, rows, xk, gu, xr, act, prodf, ps, pr, vs, vr, ob, ret, tb,
-    wny, wnb, pb, gxr, gs1, gr1, gs2, gr2, gs3, gr3, gt, gtt, gtf, wkt, wk, m, zs, zr,
+    wny, wnb, pb, gxr, gs1, gr1, gs2, gr2, gs3, gr3, gt, kt, kf, m, zs, zr,
     send_sem, recv_sem, local_sem,
 ):
     e = lax.axis_index("exp")
@@ -98,8 +98,9 @@
         copy.start()
 
     barrier = pltpu.get_barrier_semaphore()
-    peers = [at(dy=dy, dz=dz) for dy in range(4) for dz in (0, 1, -1, 2, -2, 3, -3) if dy or dz]
-    peers += [at(dz=4), at(other=True)] + [at_x(d) for d in (1, 2, 3)]
+    peers = [at(dy=d, hop=-j) for d in range(4) for j in range(4) if d or j]
+    peers += [at(dy=d, hop=1) for d in range(4)] + [at(hop=2), at(dz=4), at(other=True)]
+    peers += [at_x(d) for d in (1, 2, 3)]
     for peer in peers:
         pl.semaphore_signal(barrier, inc=1, device_id=peer, device_id_type=MESH)
 
@@ -230,19 +231,20 @@
                 wn_z[j].wait_recv()
             blocks = [(wnb[j, d] if j else wny[d, 0]).astype(F32) for d in range(4)]
             order = [blocks[(d + 4 - g) % 4][d * 8:d * 8 + 8] for g in range(4) for d in range(4)]
-            wkt[j] = jnp.concatenate(order, axis=0).T.reshape(8, 2, 32, 128).astype(BF)
-            wk[j, :, :, 0:128] = wkt[j, :, c]
-        swap.append(copy_to(wkt.at[:, :, 1 - c], wk.at[:, :, :, other_k], at(other=True)))
+            kt[j] = jnp.concatenate(order, axis=0).T.reshape(8, 2, 32, 128).astype(BF)
+            kf[j, :, :, 0:128] = kt[j, :, c]
 
     def gram_3():
         for copy in gram["x"]:
             copy.wait_recv()
-        gtt[...] = gt[...].reshape(128, 512).astype(F32).T.reshape(8, 2, 32, 128).astype(BF)
-        gtf[:, :, 0:128] = gtt[:, c]
-        swap.append(copy_to(gtt.at[:, 1 - c], gtf.at[:, :, other_k], at(other=True)))
+        kt[4] = gt[...].reshape(128, 512).astype(F32).T.reshape(8, 2, 32, 128).astype(BF)
+        kf[4, :, :, 0:128] = kt[4, :, c]
+        swap.append(copy_to(kt.at[:, :, 1 - c], kf.at[:, :, :, other_k], at(other=True)))
 
     to_x, act_x, back_core, back_pair, back_z, round_y, far_y, whole = {}, {}, {}, {}, {}, {}, {}, {}
     parts = ((0, 4), (1024, 3))
+
+    joint = {1: pl.ds(0, 2), 2: pl.ds(2, 1), 3: pl.ds(3, 1)}
 
     def spans(j):
         return parts if j == 3 else ((0, 7),)
@@ -320,9 +322,10 @@
             back_pair[j, first].wait_recv()
             tiles(count, 256, step, first)
             cols = pl.ds(first, count * 256)
-            round_y[j, first] = [
-                copy_to(ob.at[j, 0, 0, :, cols], ob.at[j, 0, g, :, cols], at(dy=g)) for g in (1, 3)
-            ]
+            if j:
+                round_y[j, first] = [
+                    copy_to(ob.at[joint[j], 0, 0, :, cols], ob.at[joint[j], 0, g, :, cols], at(dy=g)) for g in (1, 3)
+                ]
         if j:
             back_z[j] = copy_to(ob.at[j, 0, 0], ret.at[j], at(hop=-j))
 
@@ -334,7 +337,7 @@
             for side, (g, rows_g, dy) in enumerate(((1, low, 1), (3, high, -1))):
                 round_y[j, first][side].wait_recv()
                 far_y[j, first].append(
-                    copy_to(ob.at[j, 0, g, rows_g, cols], ob.at[j, 0, 2, rows_g, cols], at(dy=dy))
+                    copy_to(ob.at[joint[j], 0, g, rows_g, cols], ob.at[joint[j], 0, 2, rows_g, cols], at(dy=dy))
                 )
 
     def far(j):
@@ -342,19 +345,21 @@
             for copy in far_y[j, first]:
                 copy.wait_recv()
             cols = pl.ds(first, count * 256)
-            whole[j, first] = copy_to(ob.at[j, 0, :, :, cols], ob.at[j, 1, :, :, cols], at(other=True))
+            whole[j, first] = copy_to(
+                ob.at[joint[j], 0, :, :, cols], ob.at[joint[j], 1, :, :, cols], at(other=True)
+            )
 
     def product(j, cols):
-        return dot(wk[j].reshape(256, 256), ob[j, :, :, :, cols].reshape(256, 256))
+        return dot(kf[j].reshape(256, 256), ob[j, :, :, :, cols].reshape(256, 256))
 
     def student():
         for copy in swap:
             copy.wait_recv()
-        for j in range(3):
+        for j in (1, 2):
             whole[j, 0].wait_recv()
 
         def step(cols):
-            part = dot(gtf[...].reshape(256, 256), pb[:, :, :, cols].reshape(256, 256))
+            part = dot(kf[4].reshape(256, 256), pb[:, :, :, cols].reshape(256, 256))
             part -= product(0, cols) + product(1, cols) + product(2, cols)
             m[:, :, cols] = part.reshape(8, 32, 256)
 
@@ -381,9 +386,9 @@
         when(wn_rows), (arrive, 3), (arrive_via, 2), when(gram_0), (activate, 0), (gate_up, 1), (gate_up, 2),
         (wn_send, 2), (down, 0), when(send_proj), (arrive_via, 3), (activate, 1), (core_sum, 0), (wn_send, 3),
         (gate_up, 3), (down, 1), (activate, 2), (core_sum, 1), when(gram_1), (pair_sum, 0), (wn_send, 0),
-        (activate, 3), (down, 2), (wn_send, 1), when(swap_proj), (pair_sum, 1), (core_sum, 2), (down, 3), (relay, 0),
-        (core_sum, 3), (relay, 1), when(gram_1b), (pair_sum, 2), (far, 0), (pair_sum, 3), when(student_rows),
-        (far, 1), (relay, 2), when(gram_2), (relay, 3), (far, 2), when(gram_3), (far, 3), when(student),
+        (activate, 3), (down, 2), (wn_send, 1), when(swap_proj), (pair_sum, 1), (core_sum, 2), (down, 3),
+        (core_sum, 3), when(gram_1b), (pair_sum, 2), (relay, 1), (pair_sum, 3), when(student_rows), (relay, 2),
+        (far, 1), when(gram_2), (relay, 3), (far, 2), when(gram_3), (far, 3), when(student),
     ])
 
     to_owner = []
@@ -512,10 +517,8 @@
             pltpu.VMEM((4, 32, 512), BF),
             pltpu.VMEM((4, 32, 512), BF),
             pltpu.VMEM((4, 32, 512), BF),
-            pltpu.VMEM((8, 2, 32, 128), BF),
-            pltpu.VMEM((8, 32, 256), BF),
-            pltpu.VMEM((4, 8, 2, 32, 128), BF),
-            pltpu.VMEM((4, 8, 32, 256), BF),
+            pltpu.VMEM((5, 8, 2, 32, 128), BF),
+            pltpu.VMEM((5, 8, 32, 256), BF),
             pltpu.VMEM((8, 32, W), F32),
             pltpu.VMEM((8, 32, W), BF),
             pltpu.VMEM((8, 32, W), BF),

time: 92 us -> 92.7 us (level)
  no operation moved by 1% of the time
where the time goes in v7:
time: 92.7 us; the launch traced here: 92.5 us
  Pallas kernels  89 us (96%)
  local copies, waits for them, and re-layouts  2.89 us (3%)
    pallas_call x1, Pallas kernels, body(): pl.pallas_call(kernel, out_shape=(jax.ShapeDtypeStruct((256, W), BF), jax...  89 us
    unnamed x4, local copies, waits for them, and re-layouts  2.89 us

profile of v7, /device:TPU:1, one launch (start us, length us, event | category | flops | bytes accessed | tf_op | source)
XLA Modules:
  0.0 92.5 jit_solution(3377703103972638694)
XLA Ops:
  0.6 89.0 %shard_map.95 = (bf16[256,1792]{1,0:T(8,128)(2,1)}, f32[32,1792]{1,0:T(8,128)}) custom-call(s32[8,256]{1,0:T(8,128)} %bitcast.2, s32[8,256]{1,0:T(8,128)} %bitcast.3, bf16[32,1792]{1,0:T(8,128)(2,1)} %proj_hbm.1, bf16[256,1792]{1,0:T(8,128)(2,1)} %teacher_hbm.1, bf16[256,2048]{1,0:T(8,128)(2,1)} %student_hbm.1, bf16[1792,512]{1,0:T(8,128)(2,1)} %wg_hbm.1, ...), custom_call_target="tpu_custom_call" | custom-call | flops 8000000000 | bytes 12000000 | tf_op jit(solution)/shard_map/pallas_call | solution.py:471
  89.6 0.0 copy-start
  89.6 2.2 %copy.12 = bf16[256,1792]{1,0:T(8,128)(2,1)} copy(bf16[256,1792]{1,0:T(8,128)(2,1)} %get-tuple-element.4) | data formatting | bytes 1835008
  91.8 0.0 copy-done
  91.8 0.7 copy.13
Async XLA Ops:
  89.6 2.2 %copy-start = (f32[32,1792]{1,0:T(8,128)S(1)}, f32[32,1792]{1,0:T(8,128)}, u32[]{:S(2)}) copy-start(f32[32,1792]{1,0:T(8,128)} %get-tuple-element.5) | copy-start | bytes 688132

commit v8 on v4

--- a/solution.py
+++ b/solution.py
@@ -230,7 +230,7 @@
                 wn_z[j].wait_recv()
             blocks = [(wnb[j, d] if j else wny[d, 0]).astype(F32) for d in range(4)]
             order = [blocks[(d + 4 - g) % 4][d * 8:d * 8 + 8] for g in range(4) for d in range(4)]
-            wkt[j] = jnp.concatenate(order, axis=0).T.reshape(8, 2, 32, 128).astype(BF)
+            wkt[j] = (-jnp.concatenate(order, axis=0)).T.reshape(8, 2, 32, 128).astype(BF)
             wk[j, :, :, 0:128] = wkt[j, :, c]
         swap.append(copy_to(wkt.at[:, :, 1 - c], wk.at[:, :, :, other_k], at(other=True)))
 
@@ -344,28 +344,21 @@
             cols = pl.ds(first, count * 256)
             whole[j, first] = copy_to(ob.at[j, 0, :, :, cols], ob.at[j, 1, :, :, cols], at(other=True))
 
-    def product(j, cols):
-        return dot(wk[j].reshape(256, 256), ob[j, :, :, :, cols].reshape(256, 256))
-
-    def student():
-        for copy in swap:
-            copy.wait_recv()
-        for j in range(3):
-            whole[j, 0].wait_recv()
-
-        def step(cols):
-            part = dot(gtf[...].reshape(256, 256), pb[:, :, :, cols].reshape(256, 256))
-            part -= product(0, cols) + product(1, cols) + product(2, cols)
-            m[:, :, cols] = part.reshape(8, 32, 256)
-
-        tiles(7, 256, step)
-
     def finish(part):
+        if part == 0:
+            for copy in swap:
+                copy.wait_recv()
+            for j in range(3):
+                whole[j, 0].wait_recv()
         first, count = parts[part]
         whole[3, first].wait_recv()
 
         def step(cols):
-            m[:, :, cols] -= product(3, cols).reshape(8, 32, 256)
+            left = [wk[j].reshape(256, 256) for j in range(4)] + [gtf[...].reshape(256, 256)]
+            right = [ob[j, :, :, :, cols].reshape(256, 256) for j in range(4)]
+            right.append(pb[:, :, :, cols].reshape(256, 256))
+            out = dot(jnp.concatenate(left, axis=1), jnp.concatenate(right, axis=0))
+            m[:, :, cols] = out.reshape(8, 32, 256)
 
         tiles(count, 256, step, first)
 
@@ -383,7 +376,7 @@
         (gate_up, 3), (down, 1), (activate, 2), (core_sum, 1), when(gram_1), (pair_sum, 0), (wn_send, 0),
         (activate, 3), (down, 2), (wn_send, 1), when(swap_proj), (pair_sum, 1), (core_sum, 2), (down, 3), (relay, 0),
         (core_sum, 3), (relay, 1), when(gram_1b), (pair_sum, 2), (far, 0), (pair_sum, 3), when(student_rows),
-        (far, 1), (relay, 2), when(gram_2), (relay, 3), (far, 2), when(gram_3), (far, 3), when(student),
+        (far, 1), (relay, 2), when(gram_2), (relay, 3), (far, 2), when(gram_3), (far, 3),
     ])
 
     to_owner = []

time: 92 us -> 91.5 us (level)
  no operation moved by 1% of the time
where the time goes in v8:
time: 91.5 us; the launch traced here: 91.4 us
  Pallas kernels  87.8 us (96%)
  local copies, waits for them, and re-layouts  2.89 us (3%)
    pallas_call x1, Pallas kernels, body(): pl.pallas_call(kernel, out_shape=(jax.ShapeDtypeStruct((256, W), BF), jax...  87.8 us
    unnamed x4, local copies, waits for them, and re-layouts  2.89 us

profile of v8, /device:TPU:1, one launch (start us, length us, event | category | flops | bytes accessed | tf_op | source)
XLA Modules:
  0.0 91.4 jit_solution(3010667221371913505)
XLA Ops:
  0.6 87.8 %shard_map.95 = (bf16[256,1792]{1,0:T(8,128)(2,1)}, f32[32,1792]{1,0:T(8,128)}) custom-call(s32[8,256]{1,0:T(8,128)} %bitcast.2, s32[8,256]{1,0:T(8,128)} %bitcast.3, bf16[32,1792]{1,0:T(8,128)(2,1)} %proj_hbm.1, bf16[256,1792]{1,0:T(8,128)(2,1)} %teacher_hbm.1, bf16[256,2048]{1,0:T(8,128)(2,1)} %student_hbm.1, bf16[1792,512]{1,0:T(8,128)(2,1)} %wg_hbm.1, ...), custom_call_target="tpu_custom_call" | custom-call | flops 8000000000 | bytes 12000000 | tf_op jit(solution)/shard_map/pallas_call | solution.py:459
  88.5 0.0 copy-start
  88.5 2.2 %copy.12 = bf16[256,1792]{1,0:T(8,128)(2,1)} copy(bf16[256,1792]{1,0:T(8,128)(2,1)} %get-tuple-element.4) | data formatting | bytes 1835008
  90.7 0.0 copy-done
  90.7 0.7 copy.13
Async XLA Ops:
  88.5 2.2 %copy-start = (f32[32,1792]{1,0:T(8,128)S(1)}, f32[32,1792]{1,0:T(8,128)}, u32[]{:S(2)}) copy-start(f32[32,1792]{1,0:T(8,128)} %get-tuple-element.5) | copy-start | bytes 688132

commit v9 on v8

--- a/solution.py
+++ b/solution.py
@@ -242,7 +242,7 @@
         swap.append(copy_to(gtt.at[:, 1 - c], gtf.at[:, :, other_k], at(other=True)))
 
     to_x, act_x, back_core, back_pair, back_z, round_y, far_y, whole = {}, {}, {}, {}, {}, {}, {}, {}
-    parts = ((0, 4), (1024, 3))
+    parts = ((0, 3), (768, 2), (1280, 2))
 
     def spans(j):
         return parts if j == 3 else ((0, 7),)
@@ -423,9 +423,9 @@
         if step == 0:
             send_target()
         if step == 1:
-            for copy in started[:-8]:
+            for copy in started[:-10]:
                 copy.wait_send()
-            del started[:-8]
+            del started[:-10]
         if step == 2:
             for copy in to_owner:
                 copy.wait_recv()
@@ -451,7 +451,7 @@
     grad_out.wait()
 
 
-N_COPIES = 140
+N_COPIES = 180
 
 
 def body(teacher_in, expert_ids, gate_codes, w_gate, w_up, w_down, student_in, projection):

time: 91.5 us -> 92 us (level)
  no operation moved by 1% of the time
where the time goes in v9:
time: 92 us; the launch traced here: 91.9 us
  Pallas kernels  88.4 us (96%)
  local copies, waits for them, and re-layouts  2.89 us (3%)
    pallas_call x1, Pallas kernels, body(): pl.pallas_call(kernel, out_shape=(jax.ShapeDtypeStruct((256, W), BF), jax...  88.4 us
    unnamed x4, local copies, waits for them, and re-layouts  2.89 us

profile of v9, /device:TPU:1, one launch (start us, length us, event | category | flops | bytes accessed | tf_op | source)
XLA Modules:
  0.0 91.9 jit_solution(8048367754423440091)
XLA Ops:
  0.6 88.4 %shard_map.95 = (bf16[256,1792]{1,0:T(8,128)(2,1)}, f32[32,1792]{1,0:T(8,128)}) custom-call(s32[8,256]{1,0:T(8,128)} %bitcast.2, s32[8,256]{1,0:T(8,128)} %bitcast.3, bf16[32,1792]{1,0:T(8,128)(2,1)} %proj_hbm.1, bf16[256,1792]{1,0:T(8,128)(2,1)} %teacher_hbm.1, bf16[256,2048]{1,0:T(8,128)(2,1)} %student_hbm.1, bf16[1792,512]{1,0:T(8,128)(2,1)} %wg_hbm.1, ...), custom_call_target="tpu_custom_call" | custom-call | flops 8000000000 | bytes 12000000 | tf_op jit(solution)/shard_map/pallas_call | solution.py:459
  89.0 0.0 copy-start
  89.0 2.2 %copy.12 = bf16[256,1792]{1,0:T(8,128)(2,1)} copy(bf16[256,1792]{1,0:T(8,128)(2,1)} %get-tuple-element.4) | data formatting | bytes 1835008
  91.2 0.0 copy-done
  91.2 0.7 copy.13
Async XLA Ops:
  89.0 2.2 %copy-start = (f32[32,1792]{1,0:T(8,128)S(1)}, f32[32,1792]{1,0:T(8,128)}, u32[]{:S(2)}) copy-start(f32[32,1792]{1,0:T(8,128)} %get-tuple-element.5) | copy-start | bytes 688132

commit v10 on v8

--- a/solution.py
+++ b/solution.py
@@ -98,8 +98,9 @@
         copy.start()
 
     barrier = pltpu.get_barrier_semaphore()
-    peers = [at(dy=dy, dz=dz) for dy in range(4) for dz in (0, 1, -1, 2, -2, 3, -3) if dy or dz]
-    peers += [at(dz=4), at(other=True)] + [at_x(d) for d in (1, 2, 3)]
+    peers = [at(dy=d, hop=-j) for d in range(4) for j in range(4) if d or j]
+    peers += [at(dy=d, hop=1) for d in range(4)] + [at(hop=2), at(dz=4), at(other=True)]
+    peers += [at_x(d) for d in (1, 2, 3)]
     for peer in peers:
         pl.semaphore_signal(barrier, inc=1, device_id=peer, device_id_type=MESH)
 
@@ -420,13 +421,13 @@
                         zs[slot, :, cols] = (mine(far, 0, 32, cols) + zr[slot - 2, :, cols].astype(F32)).astype(BF)
                     src, dst = zs.at[slot, :, cols], zr.at[slot, :, cols]
                 hops[step, half, way] = copy_to(src, dst, at(dz=sign))
-        if step == 0:
+        if step == 1:
             send_target()
-        if step == 1:
-            for copy in started[:-8]:
+        if step == 2:
+            for copy in started[:-12]:
                 copy.wait_send()
-            del started[:-8]
-        if step == 2:
+            del started[:-12]
+        if step == 3:
             for copy in to_owner:
                 copy.wait_recv()
 

time: 91.5 us -> 92.2 us (level)
  no operation moved by 1% of the time
where the time goes in v10:
time: 92.2 us; the launch traced here: 92.1 us
  Pallas kernels  88.6 us (96%)
  local copies, waits for them, and re-layouts  2.89 us (3%)
    pallas_call x1, Pallas kernels, body(): pl.pallas_call(kernel, out_shape=(jax.ShapeDtypeStruct((256, W), BF), jax...  88.6 us
    unnamed x4, local copies, waits for them, and re-layouts  2.89 us

profile of v10, /device:TPU:1, one launch (start us, length us, event | category | flops | bytes accessed | tf_op | source)
XLA Modules:
  0.0 92.1 jit_solution(6518689686339219924)
XLA Ops:
  0.6 88.6 %shard_map.95 = (bf16[256,1792]{1,0:T(8,128)(2,1)}, f32[32,1792]{1,0:T(8,128)}) custom-call(s32[8,256]{1,0:T(8,128)} %bitcast.2, s32[8,256]{1,0:T(8,128)} %bitcast.3, bf16[32,1792]{1,0:T(8,128)(2,1)} %proj_hbm.1, bf16[256,1792]{1,0:T(8,128)(2,1)} %teacher_hbm.1, bf16[256,2048]{1,0:T(8,128)(2,1)} %student_hbm.1, bf16[1792,512]{1,0:T(8,128)(2,1)} %wg_hbm.1, ...), custom_call_target="tpu_custom_call" | custom-call | flops 8000000000 | bytes 12000000 | tf_op jit(solution)/shard_map/pallas_call | solution.py:460
  89.2 0.0 copy-start
  89.2 2.2 %copy.12 = bf16[256,1792]{1,0:T(8,128)(2,1)} copy(bf16[256,1792]{1,0:T(8,128)(2,1)} %get-tuple-element.4) | data formatting | bytes 1835008
  91.4 0.0 copy-done
  91.4 0.7 copy.13
Async XLA Ops:
  89.2 2.2 %copy-start = (f32[32,1792]{1,0:T(8,128)S(1)}, f32[32,1792]{1,0:T(8,128)}, u32[]{:S(2)}) copy-start(f32[32,1792]{1,0:T(8,128)} %get-tuple-element.5) | copy-start | bytes 688132
